TPU v7x, 32 devices: a whole 2x2x4 slice. The times are simulated.
32 devices in a mesh: fsdp: 32 (over z, y, x, core).
Axes of the slice: x: 2, y: 2, z: 4, core: 2. Of those that a mesh axis runs over, the one named last changes fastest.
Arguments:
- tokens: bfloat16 [8192, 768], P('fsdp'), may hold values from -6 to 6
- cotangent: bfloat16 [8192, 768], P('fsdp'), may hold values from -6 to 6
- counts: int32 [32], P('fsdp'), may hold values from 1 to 2, as said below
- ln1_gain: bfloat16 [768], P('fsdp'), may hold values from 0.099609375 to 1.8984375
- ln1_bias: bfloat16 [768], P('fsdp'), may hold values from -4 to 4
- w_query: bfloat16 [768, 768], P('fsdp'), may hold values from -0.3125 to 0.3125
- b_query: bfloat16 [768], P('fsdp'), may hold values from -4 to 4
- w_key: bfloat16 [768, 768], P('fsdp'), may hold values from -0.3125 to 0.3125
- w_value: bfloat16 [768, 768], P('fsdp'), may hold values from -0.21875 to 0.21875
- b_value: bfloat16 [768], P('fsdp'), may hold values from -4 to 4
- w_out: bfloat16 [768, 768], P('fsdp'), may hold values from -0.625 to 0.625
- b_out: bfloat16 [768], P('fsdp'), may hold values from -4 to 4
- ln2_gain: bfloat16 [768], P('fsdp'), may hold values from 0.099609375 to 1.8984375
- ln2_bias: bfloat16 [768], P('fsdp'), may hold values from -4 to 4
- w_fc1: bfloat16 [768, 3072], P('fsdp'), may hold values from -0.21875 to 0.21875
- b_fc1: bfloat16 [3072], P('fsdp'), may hold values from -4 to 4
- w_fc2: bfloat16 [3072, 768], P('fsdp'), may hold values from -0.15625 to 0.15625
- b_fc2: bfloat16 [768], P('fsdp'), may hold values from -4 to 4
Outputs:
- mixed: bfloat16 [8192, 768], P('fsdp')
- grad_tokens: float32 [8192, 768], P('fsdp')
- grad_ln1_gain: float32 [768], P('fsdp')
- grad_ln1_bias: float32 [768], P('fsdp')
- grad_w_query: float32 [768, 768], P('fsdp')
- grad_b_query: float32 [768], P('fsdp')
- grad_w_key: float32 [768, 768], P('fsdp')
- grad_w_value: float32 [768, 768], P('fsdp')
- grad_b_value: float32 [768], P('fsdp')
- grad_w_out: float32 [768, 768], P('fsdp')
- grad_b_out: float32 [768], P('fsdp')
- grad_ln2_gain: float32 [768], P('fsdp')
- grad_ln2_bias: float32 [768], P('fsdp')
- grad_w_fc1: float32 [768, 3072], P('fsdp')
- grad_b_fc1: float32 [3072], P('fsdp')
- grad_w_fc2: float32 [3072, 768], P('fsdp')
- grad_b_fc2: float32 [768], P('fsdp')
Inputs may be any that keep to these rules, and one draw needn't show every extreme that they name: `counts`: some device has 2 live micro-batches and another has one.
All inputs are finite; a program needn't handle non-finite values.
Results may differ from a plain program's by a relative error of at most 0.013.
The roundings to bfloat16 on the way count: a program that leaves them out, or rounds other values in their place, can miss the bound.
Values may be sent and summed in bfloat16 or wider, within the bound.
A program may use at most 192 MiB of HBM per device.

v0:
```python
import jax
import jax.numpy as jnp
from jax import lax
from jax.sharding import PartitionSpec as P

HD = 64
LENGTH = 128


EPS = 1e-05
BF = jnp.bfloat16
FL = jnp.float32


def normalize(values, gain, shift):
    center = values - jnp.mean(values, -1, keepdims=True)
    spread = jnp.mean(center * center, -1, keepdims=True)
    inverse = lax.rsqrt(spread + EPS)
    plain = center * inverse
    return (plain * gain.astype(FL) + shift.astype(FL), plain, inverse)


def norm_back(grad, plain, inverse, gain):
    scaled = grad * gain.astype(FL)
    inner = (
        scaled
        - jnp.mean(scaled, -1, keepdims=True)
        - plain * jnp.mean(scaled * plain, -1, keepdims=True)
    )
    return (inverse * inner, jnp.sum(grad * plain, 0), jnp.sum(grad, 0))


def project(left, right):
    return jnp.dot(left, right, preferred_element_type=FL)


def back_project(grad, right):
    return jnp.einsum("te,de->td", grad, right, preferred_element_type=FL)


def outer_sum(left, grad):
    return jnp.einsum("td,te->de", left, grad, preferred_element_type=FL)


def run_forward(rows, params):
    (
        ln1_gain,
        ln1_bias,
        w_query,
        b_query,
        w_key,
        w_value,
        b_value,
        w_out,
        b_out,
        ln2_gain,
        ln2_bias,
        w_fc1,
        b_fc1,
        w_fc2,
        b_fc2,
    ) = params
    length, width = rows.shape
    heads = width // HD
    inputs = rows.astype(FL)
    normed_full, plain_one, inverse_one = normalize(inputs, ln1_gain, ln1_bias)
    normed = normed_full.astype(BF)
    queries = (project(normed, w_query) + b_query.astype(FL)).astype(BF).reshape(length, heads, HD)
    key_rows = project(normed, w_key).astype(BF).reshape(length, heads, HD)
    value_rows = (
        (project(normed, w_value) + b_value.astype(FL)).astype(BF).reshape(length, heads, HD)
    )
    scores = jnp.einsum("qhd,khd->hqk", queries, key_rows, preferred_element_type=FL) * HD ** (-0.5)
    causal = jnp.arange(length)[:, None] >= jnp.arange(length)[None, :]
    scores = jnp.where(causal, scores, -1e30)
    highest = jnp.max(scores, -1, keepdims=True)
    expo = jnp.exp(scores - highest)
    probs = expo / jnp.sum(expo, -1, keepdims=True)
    weights = probs.astype(BF)
    attended = jnp.einsum("hqk,khd->qhd", weights, value_rows, preferred_element_type=FL)
    attended = attended.reshape(length, width).astype(BF)
    middle = inputs + project(attended, w_out) + b_out.astype(FL)
    normed_two_full, plain_two, inverse_two = normalize(middle, ln2_gain, ln2_bias)
    normed_two = normed_two_full.astype(BF)
    hidden_pre = project(normed_two, w_fc1) + b_fc1.astype(FL)
    activated = jax.nn.gelu(hidden_pre).astype(BF)
    result = middle + project(activated, w_fc2) + b_fc2.astype(FL)
    kept = (
        normed,
        plain_one,
        inverse_one,
        queries,
        key_rows,
        value_rows,
        probs,
        weights,
        attended,
        plain_two,
        inverse_two,
        normed_two,
        hidden_pre,
        activated,
    )
    return (result, kept)


def run_backward(rows, grad_rows, params):
    (
        ln1_gain,
        ln1_bias,
        w_query,
        b_query,
        w_key,
        w_value,
        b_value,
        w_out,
        b_out,
        ln2_gain,
        ln2_bias,
        w_fc1,
        b_fc1,
        w_fc2,
        b_fc2,
    ) = params
    length, width = rows.shape
    heads = width // HD
    unused, kept = run_forward(rows, params)
    (
        normed,
        plain_one,
        inverse_one,
        queries,
        key_rows,
        value_rows,
        probs,
        weights,
        attended,
        plain_two,
        inverse_two,
        normed_two,
        hidden_pre,
        activated,
    ) = kept
    grad_out = grad_rows.astype(FL)
    grad_b_fc2 = jnp.sum(grad_out, 0)
    grad_w_fc2 = outer_sum(activated, grad_rows)
    grad_act = back_project(grad_rows, w_fc2)
    unused_value, gelu_pull = jax.vjp(jax.nn.gelu, hidden_pre)
    grad_pre = gelu_pull(grad_act)[0].astype(BF)
    grad_b_fc1 = jnp.sum(grad_pre.astype(FL), 0)
    grad_w_fc1 = outer_sum(normed_two, grad_pre)
    grad_norm_two = back_project(grad_pre, w_fc1)
    through_two, grad_ln2_gain, grad_ln2_bias = norm_back(
        grad_norm_two, plain_two, inverse_two, ln2_gain
    )
    grad_middle = grad_out + through_two
    grad_branch = grad_middle.astype(BF)
    grad_b_out = jnp.sum(grad_branch.astype(FL), 0)
    grad_w_out = outer_sum(attended, grad_branch)
    grad_att = back_project(grad_branch, w_out).astype(BF).reshape(length, heads, HD)
    grad_probs = jnp.einsum("qhd,khd->hqk", grad_att, value_rows, preferred_element_type=FL)
    grad_values = jnp.einsum("hqk,qhd->khd", weights, grad_att, preferred_element_type=FL)
    grad_values = grad_values.astype(BF).reshape(length, width)
    grad_scores = probs * (grad_probs - jnp.sum(probs * grad_probs, -1, keepdims=True))
    grad_scores = grad_scores.astype(BF)
    grad_queries = jnp.einsum(
        "hqk,khd->qhd", grad_scores, key_rows, preferred_element_type=FL
    ) * HD ** (-0.5)
    grad_keys = jnp.einsum(
        "hqk,qhd->khd", grad_scores, queries, preferred_element_type=FL
    ) * HD ** (-0.5)
    grad_queries = grad_queries.astype(BF).reshape(length, width)
    grad_keys = grad_keys.astype(BF).reshape(length, width)
    grad_b_query = jnp.sum(grad_queries.astype(FL), 0)
    grad_b_value = jnp.sum(grad_values.astype(FL), 0)
    grad_w_query = outer_sum(normed, grad_queries)
    grad_w_key = outer_sum(normed, grad_keys)
    grad_w_value = outer_sum(normed, grad_values)
    grad_norm_one = (
        back_project(grad_queries, w_query)
        + back_project(grad_keys, w_key)
        + back_project(grad_values, w_value)
    )
    through_one, grad_ln1_gain, grad_ln1_bias = norm_back(
        grad_norm_one, plain_one, inverse_one, ln1_gain
    )
    grad_inputs = grad_middle + through_one
    grads = (
        grad_ln1_gain,
        grad_ln1_bias,
        grad_w_query,
        grad_b_query,
        grad_w_key,
        grad_w_value,
        grad_b_value,
        grad_w_out,
        grad_b_out,
        grad_ln2_gain,
        grad_ln2_bias,
        grad_w_fc1,
        grad_b_fc1,
        grad_w_fc2,
        grad_b_fc2,
    )
    return (grad_inputs, grads)


def on_device(
    tokens,
    cotangent,
    counts,
    ln1_gain,
    ln1_bias,
    w_query,
    b_query,
    w_key,
    w_value,
    b_value,
    w_out,
    b_out,
    ln2_gain,
    ln2_bias,
    w_fc1,
    b_fc1,
    w_fc2,
    b_fc2,
):
    shards = (
        ln1_gain,
        ln1_bias,
        w_query,
        b_query,
        w_key,
        w_value,
        b_value,
        w_out,
        b_out,
        ln2_gain,
        ln2_bias,
        w_fc1,
        b_fc1,
        w_fc2,
        b_fc2,
    )
    devices = lax.axis_size("fsdp")
    width = tokens.shape[1]
    slots = tokens.shape[0] // LENGTH
    token_slots = tokens.reshape(slots, LENGTH, width)
    cot_slots = cotangent.reshape(slots, LENGTH, width)
    limit = counts[0]
    zero_grads = tuple(
        (jnp.zeros((piece.shape[0] * devices,) + piece.shape[1:], FL) for piece in shards)
    )

    def per_slot(totals, pieces):
        slot_tokens, slot_cot, slot = pieces
        active = slot < limit
        forward_params = (
            lax.all_gather(ln1_gain, "fsdp", axis=0, tiled=True),
            lax.all_gather(ln1_bias, "fsdp", axis=0, tiled=True),
            lax.all_gather(w_query, "fsdp", axis=0, tiled=True),
            lax.all_gather(b_query, "fsdp", axis=0, tiled=True),
            lax.all_gather(w_key, "fsdp", axis=0, tiled=True),
            lax.all_gather(w_value, "fsdp", axis=0, tiled=True),
            lax.all_gather(b_value, "fsdp", axis=0, tiled=True),
            lax.all_gather(w_out, "fsdp", axis=0, tiled=True),
            lax.all_gather(b_out, "fsdp", axis=0, tiled=True),
            lax.all_gather(ln2_gain, "fsdp", axis=0, tiled=True),
            lax.all_gather(ln2_bias, "fsdp", axis=0, tiled=True),
            lax.all_gather(w_fc1, "fsdp", axis=0, tiled=True),
            lax.all_gather(b_fc1, "fsdp", axis=0, tiled=True),
            lax.all_gather(w_fc2, "fsdp", axis=0, tiled=True),
            lax.all_gather(b_fc2, "fsdp", axis=0, tiled=True),
        )

        def forward_live(rows):
            return run_forward(rows, forward_params)[0].astype(BF)

        def forward_dead(rows):
            return jnp.zeros_like(rows)

        outputs = lax.cond(active, forward_live, forward_dead, slot_tokens)
        backward_params = (
            lax.all_gather(ln1_gain, "fsdp", axis=0, tiled=True),
            lax.all_gather(ln1_bias, "fsdp", axis=0, tiled=True),
            lax.all_gather(w_query, "fsdp", axis=0, tiled=True),
            lax.all_gather(b_query, "fsdp", axis=0, tiled=True),
            lax.all_gather(w_key, "fsdp", axis=0, tiled=True),
            lax.all_gather(w_value, "fsdp", axis=0, tiled=True),
            lax.all_gather(b_value, "fsdp", axis=0, tiled=True),
            lax.all_gather(w_out, "fsdp", axis=0, tiled=True),
            lax.all_gather(b_out, "fsdp", axis=0, tiled=True),
            lax.all_gather(ln2_gain, "fsdp", axis=0, tiled=True),
            lax.all_gather(ln2_bias, "fsdp", axis=0, tiled=True),
            lax.all_gather(w_fc1, "fsdp", axis=0, tiled=True),
            lax.all_gather(b_fc1, "fsdp", axis=0, tiled=True),
            lax.all_gather(w_fc2, "fsdp", axis=0, tiled=True),
            lax.all_gather(b_fc2, "fsdp", axis=0, tiled=True),
        )

        def backward_live(pair):
            return run_backward(pair[0], pair[1], backward_params)

        def backward_dead(pair):
            return (jnp.zeros(pair[0].shape, FL), zero_grads)

        grad_inputs, grads = lax.cond(active, backward_live, backward_dead, (slot_tokens, slot_cot))
        totals = jax.tree.map(jnp.add, totals, grads)
        return (totals, (outputs, grad_inputs))

    totals, (out_slots, grad_slots) = lax.scan(
        per_slot, zero_grads, (token_slots, cot_slots, jnp.arange(slots, dtype=jnp.int32))
    )
    (
        sum_ln1_gain,
        sum_ln1_bias,
        sum_w_query,
        sum_b_query,
        sum_w_key,
        sum_w_value,
        sum_b_value,
        sum_w_out,
        sum_b_out,
        sum_ln2_gain,
        sum_ln2_bias,
        sum_w_fc1,
        sum_b_fc1,
        sum_w_fc2,
        sum_b_fc2,
    ) = totals
    owned = (
        lax.psum_scatter(sum_ln1_gain, "fsdp", scatter_dimension=0, tiled=True),
        lax.psum_scatter(sum_ln1_bias, "fsdp", scatter_dimension=0, tiled=True),
        lax.psum_scatter(sum_w_query, "fsdp", scatter_dimension=0, tiled=True),
        lax.psum_scatter(sum_b_query, "fsdp", scatter_dimension=0, tiled=True),
        lax.psum_scatter(sum_w_key, "fsdp", scatter_dimension=0, tiled=True),
        lax.psum_scatter(sum_w_value, "fsdp", scatter_dimension=0, tiled=True),
        lax.psum_scatter(sum_b_value, "fsdp", scatter_dimension=0, tiled=True),
        lax.psum_scatter(sum_w_out, "fsdp", scatter_dimension=0, tiled=True),
        lax.psum_scatter(sum_b_out, "fsdp", scatter_dimension=0, tiled=True),
        lax.psum_scatter(sum_ln2_gain, "fsdp", scatter_dimension=0, tiled=True),
        lax.psum_scatter(sum_ln2_bias, "fsdp", scatter_dimension=0, tiled=True),
        lax.psum_scatter(sum_w_fc1, "fsdp", scatter_dimension=0, tiled=True),
        lax.psum_scatter(sum_b_fc1, "fsdp", scatter_dimension=0, tiled=True),
        lax.psum_scatter(sum_w_fc2, "fsdp", scatter_dimension=0, tiled=True),
        lax.psum_scatter(sum_b_fc2, "fsdp", scatter_dimension=0, tiled=True),
    )
    mixed = out_slots.reshape(tokens.shape)
    grad_tokens = grad_slots.reshape(tokens.shape[0], width)
    return (mixed, grad_tokens) + tuple(owned)


def solution(mesh):
    in_specs = (
        P("fsdp", None),
        P("fsdp", None),
        P("fsdp"),
        P("fsdp"),
        P("fsdp"),
        P("fsdp", None),
        P("fsdp"),
        P("fsdp", None),
        P("fsdp", None),
        P("fsdp"),
        P("fsdp", None),
        P("fsdp"),
        P("fsdp"),
        P("fsdp"),
        P("fsdp", None),
        P("fsdp"),
        P("fsdp", None),
        P("fsdp"),
    )
    out_specs = (
        P("fsdp", None),
        P("fsdp", None),
        P("fsdp"),
        P("fsdp"),
        P("fsdp", None),
        P("fsdp"),
        P("fsdp", None),
        P("fsdp", None),
        P("fsdp"),
        P("fsdp", None),
        P("fsdp"),
        P("fsdp"),
        P("fsdp"),
        P("fsdp", None),
        P("fsdp"),
        P("fsdp", None),
        P("fsdp"),
    )
    return jax.shard_map(
        on_device, mesh=mesh, in_specs=in_specs, out_specs=out_specs, check_vma=False
    )
```

profile of v0, /device:TPU:0, one launch (start us, length us, event | category | flops | bytes accessed | tf_op | source)
XLA Modules:
  0.0 1635.6 jit_solution(12760920499098771753)
XLA Ops:
  8.7 871.8 %while.43 = (s32[]{:T(128)}, f32[768]{0:T(1024)}, f32[768]{0:T(1024)}, f32[768,768]{1,0:T(8,128)}, f32[768]{0:T(1024)}, /*index=5*/f32[768,768]{1,0:T(8,128)}, f...) while((s32[]{:T(128)}, f32[768]{0:T(1024)}, ...), condition=%wide.region_31.32_spmd.clone, body=%wide.region_0.31_spmd.clone.sunk | while | flops 6973463552 | bytes 347627360 | solution.py:311
  22.8 42.4 %all-reduce.30 = (bf16[768]{0:T(1024)(128)(2,1)S(1)}, bf16[768]{0:T(1024)(128)(2,1)S(1)}, bf16[768]{0:T(1024)(128)(2,1)S(1)}, bf16[768]{0:T(1024)(128)(2,1)S(1)}...) all-reduce(bf16[768]{0:T(1024)(128)(2,1)S(1)} %dynamic-update-slice, ...), channel_id=1, replica_groups=mesh['fsdp'=32] {'fsdp'}, use_global_device_ids=true, to_apply=%add | all-reduce | flops 9216 | bytes 36864 | tf_op jit(solution)/shard_map/while
  66.1 3.2 all-gather.13.cloned.1.call-done
  69.3 55.9 %all-gather.11.cloned.1.call-done = bf16[768,768]{1,0:T(8,128)(2,1)} async-done(((bf16[24,768]{1,0:T(8,128)(2,1)}), bf16[768,768]{1,0:T(8,128)(2,1)}) %all-gather.11.cloned.1.call-update) | async-done | bytes 1179664 | tf_op jit(solution)/shard_map/while/body/eval_jaxpr/all_gather | solution.py:289
  125.2 55.9 %all-gather.7.cloned.1.call-done = bf16[768,768]{1,0:T(8,128)(2,1)} async-done(((bf16[24,768]{1,0:T(8,128)(2,1)}), bf16[768,768]{1,0:T(8,128)(2,1)}) %all-gather.7.cloned.1.call-update) | async-done | bytes 1179664 | tf_op jit(solution)/shard_map/while/body/eval_jaxpr/all_gather | solution.py:288
  181.1 55.8 %all-gather.9.cloned.1.call-done = bf16[768,768]{1,0:T(8,128)(2,1)} async-done(((bf16[24,768]{1,0:T(8,128)(2,1)}), bf16[768,768]{1,0:T(8,128)(2,1)}) %all-gather.9.cloned.1.call-update) | async-done | bytes 1179664 | tf_op jit(solution)/shard_map/while/body/eval_jaxpr/all_gather | solution.py:286
  236.8 65.4 %all-gather.15.cloned.1.call-done = bf16[3072,768]{1,0:T(8,128)(2,1)} async-done(((bf16[96,768]{1,0:T(8,128)(2,1)}), bf16[3072,768]{1,0:T(8,128)(2,1)}) %all-gather.15.cloned.1.call-update) | async-done | bytes 4718608 | tf_op jit(solution)/shard_map/while/body/eval_jaxpr/all_gather | solution.py:297
  302.2 65.2 %all-gather.17.cloned.1.call-done = bf16[768,3072]{1,0:T(8,128)(2,1)} async-done(((bf16[24,3072]{1,0:T(8,128)(2,1)}), bf16[768,3072]{1,0:T(8,128)(2,1)}) %all-gather.17.cloned.1.call-update) | async-done | bytes 4718608 | tf_op jit(solution)/shard_map/while/body/eval_jaxpr/all_gather | solution.py:295
  367.4 12.3 conditional.7
  374.1 5.7 fusion.84
  380.4 53.8 %conditional.6 = (f32[768]{0:T(1024)S(1)}, f32[768]{0:T(1024)S(1)}, f32[768,768]{1,0:T(8,128)}, f32[768]{0:T(1024)S(1)}, f32[768,768]{1,0:T(8,128)}, /*index=5*/...) conditional(s32[]{:T(128)} %convert_element_type.320, () %tuple.90, ...), branch_computations={%region_1.1_spmd, %region_2.22_spmd} | conditional | flops 5061690368 | bytes 143311552 | solution.py:307
  382.1 1.6 fusion.13
  389.3 3.4 convolution_add_fusion
  392.7 4.9 convert_reduce_fusion
  397.7 2.3 multiply_reduce_fusion.1
  402.8 1.7 copy.67
  404.5 2.6 convert_reduce_fusion.4
  412.1 1.9 fusion.113
  415.8 1.8 fusion.47
  417.6 2.1 fusion.58
  419.7 2.0 fusion.60
  421.7 2.0 fusion.62
  423.8 5.2 fusion.16
  429.0 5.2 fusion.57
  435.6 10.4 select_add_fusion.30
  446.1 8.5 select_add_fusion.32
  454.9 5.3 select_add_fusion.25
  460.3 4.0 select_add_fusion.27
  480.7 40.2 %all-reduce.30 = (bf16[768]{0:T(1024)(128)(2,1)S(1)}, bf16[768]{0:T(1024)(128)(2,1)S(1)}, bf16[768]{0:T(1024)(128)(2,1)S(1)}, bf16[768]{0:T(1024)(128)(2,1)S(1)}...) all-reduce(bf16[768]{0:T(1024)(128)(2,1)S(1)} %dynamic-update-slice, ...), channel_id=1, replica_groups=mesh['fsdp'=32] {'fsdp'}, use_global_device_ids=true, to_apply=%add | all-reduce | flops 9216 | bytes 36864 | tf_op jit(solution)/shard_map/while
  523.1 55.9 %all-gather.11.cloned.1.call-done = bf16[768,768]{1,0:T(8,128)(2,1)} async-done(((bf16[24,768]{1,0:T(8,128)(2,1)}), bf16[768,768]{1,0:T(8,128)(2,1)}) %all-gather.11.cloned.1.call-update) | async-done | bytes 1179664 | tf_op jit(solution)/shard_map/while/body/eval_jaxpr/all_gather | solution.py:289
  579.0 55.9 %all-gather.7.cloned.1.call-done = bf16[768,768]{1,0:T(8,128)(2,1)} async-done(((bf16[24,768]{1,0:T(8,128)(2,1)}), bf16[768,768]{1,0:T(8,128)(2,1)}) %all-gather.7.cloned.1.call-update) | async-done | bytes 1179664 | tf_op jit(solution)/shard_map/while/body/eval_jaxpr/all_gather | solution.py:288
  634.9 55.7 %all-gather.9.cloned.1.call-done = bf16[768,768]{1,0:T(8,128)(2,1)} async-done(((bf16[24,768]{1,0:T(8,128)(2,1)}), bf16[768,768]{1,0:T(8,128)(2,1)}) %all-gather.9.cloned.1.call-update) | async-done | bytes 1179664 | tf_op jit(solution)/shard_map/while/body/eval_jaxpr/all_gather | solution.py:286
  690.7 65.5 %all-gather.15.cloned.1.call-done = bf16[3072,768]{1,0:T(8,128)(2,1)} async-done(((bf16[96,768]{1,0:T(8,128)(2,1)}), bf16[3072,768]{1,0:T(8,128)(2,1)}) %all-gather.15.cloned.1.call-update) | async-done | bytes 4718608 | tf_op jit(solution)/shard_map/while/body/eval_jaxpr/all_gather | solution.py:297
  756.2 65.2 %all-gather.17.cloned.1.call-done = bf16[768,3072]{1,0:T(8,128)(2,1)} async-done(((bf16[24,3072]{1,0:T(8,128)(2,1)}), bf16[768,3072]{1,0:T(8,128)(2,1)}) %all-gather.17.cloned.1.call-update) | async-done | bytes 4718608 | tf_op jit(solution)/shard_map/while/body/eval_jaxpr/all_gather | solution.py:295
  822.2 18.5 %conditional.6 = (f32[768]{0:T(1024)S(1)}, f32[768]{0:T(1024)S(1)}, f32[768,768]{1,0:T(8,128)}, f32[768]{0:T(1024)S(1)}, f32[768,768]{1,0:T(8,128)}, /*index=5*/...) conditional(s32[]{:T(128)} %convert_element_type.320, () %tuple.90, ...), branch_computations={%region_1.1_spmd, %region_2.22_spmd} | conditional | flops 5061690368 | bytes 143311552 | solution.py:307
  831.5 4.3 broadcast_in_dim.53
  835.8 4.8 broadcast_in_dim.51
  842.7 13.2 select_add_fusion.30
  856.1 11.2 select_add_fusion.32
  867.6 6.6 select_add_fusion.25
  874.3 4.0 select_add_fusion.27
  884.5 88.1 %all-reduce.28 = (f32[768]{0:T(1024)S(1)}, f32[768]{0:T(1024)S(1)}, f32[768]{0:T(1024)S(1)}, f32[768]{0:T(1024)S(1)}, f32[768]{0:T(1024)S(1)}, /*index=5*/f32[76...) all-reduce(f32[768]{0:T(1024)S(1)} %copy-done.76, ...), channel_id=2, replica_groups=mesh['fsdp'=32] {'fsdp'}, use_global_device_ids=true, to_apply=%region_32.33.clone | all-reduce | flops 9216 | bytes 73728
  977.9 54.1 %reduce-scatter.7.cloned.1.call-done = f32[24,768]{1,0:T(8,128)} async-done(((f32[768,768]{1,0:T(8,128)}), f32[24,768]{1,0:T(8,128)}) %reduce-scatter.7.cloned.1.call-update) | async-done | bytes 73744 | tf_op jit(solution)/shard_map/reduce_scatter | solution.py:334
  1032.0 104.5 %reduce-scatter.9.cloned.1.call-done = f32[24,768]{1,0:T(8,128)} async-done(((f32[768,768]{1,0:T(8,128)}), f32[24,768]{1,0:T(8,128)}) %reduce-scatter.9.cloned.1.call-update) | async-done | bytes 73744 | tf_op jit(solution)/shard_map/reduce_scatter | solution.py:336
  1136.5 103.7 %reduce-scatter.11.cloned.1.call-done = f32[24,768]{1,0:T(8,128)} async-done(((f32[768,768]{1,0:T(8,128)}), f32[24,768]{1,0:T(8,128)}) %reduce-scatter.11.cloned.1.call-update) | async-done | bytes 73744 | tf_op jit(solution)/shard_map/reduce_scatter | solution.py:337
  1240.2 104.8 %reduce-scatter.13.cloned.1.call-done = f32[24,768]{1,0:T(8,128)} async-done(((f32[768,768]{1,0:T(8,128)}), f32[24,768]{1,0:T(8,128)}) %reduce-scatter.13.cloned.1.call-update) | async-done | bytes 73744 | tf_op jit(solution)/shard_map/reduce_scatter | solution.py:339
  1345.0 141.1 %reduce-scatter.15.cloned.1.call-done = f32[24,3072]{1,0:T(8,128)} async-done(((f32[768,3072]{1,0:T(8,128)}), f32[24,3072]{1,0:T(8,128)}) %reduce-scatter.15.cloned.1.call-update) | async-done | bytes 294928 | tf_op jit(solution)/shard_map/reduce_scatter | solution.py:343
  1486.1 142.1 %reduce-scatter.17.cloned.1.call-done = f32[96,768]{1,0:T(8,128)} async-done(((f32[3072,768]{1,0:T(8,128)}), f32[96,768]{1,0:T(8,128)}) %reduce-scatter.17.cloned.1.call-update) | async-done | bytes 294928 | tf_op jit(solution)/shard_map/reduce_scatter | solution.py:345
  (420 shorter events, 80.0 us)
Async XLA Ops:
  8.7 60.6 %all-gather.13.cloned.1.call-start = ((), (), s32[]{:S(2)}) async-start(), calls=%async_computation.15 | async-start | bytes 1216512 | tf_op jit(solution)/shard_map/while/body/eval_jaxpr/all_gather | solution.py:291
  9.4 115.8 %all-gather.11.cloned.1.call-start = ((), (), s32[]{:S(2)}) async-start(), calls=%async_computation.14 | async-start | bytes 1216512 | tf_op jit(solution)/shard_map/while/body/eval_jaxpr/all_gather | solution.py:289
  10.2 170.9 %all-gather.7.cloned.1.call-start = ((), (), s32[]{:S(2)}) async-start(), calls=%async_computation.12 | async-start | bytes 1216512 | tf_op jit(solution)/shard_map/while/body/eval_jaxpr/all_gather | solution.py:288
  10.9 225.9 %all-gather.9.cloned.1.call-start = ((), (), s32[]{:S(2)}) async-start(), calls=%async_computation.13 | async-start | bytes 1216512 | tf_op jit(solution)/shard_map/while/body/eval_jaxpr/all_gather | solution.py:286
  11.5 290.7 %all-gather.15.cloned.1.call-start = ((), (), s32[]{:S(2)}) async-start(), calls=%async_computation.16 | async-start | bytes 4866048 | tf_op jit(solution)/shard_map/while/body/eval_jaxpr/all_gather | solution.py:297
  12.1 355.4 %all-gather.17.cloned.1.call-start = ((), (), s32[]{:S(2)}) async-start(), calls=%async_computation.17 | async-start | bytes 4866048 | tf_op jit(solution)/shard_map/while/body/eval_jaxpr/all_gather | solution.py:295
  389.1 10.9 copy-start.28
  389.3 10.7 copy-start.47
  446.0 8.7 copy-start.38
  446.0 8.7 copy-start.41
  446.0 8.7 copy-start.65
  446.0 8.7 copy-start.68
  446.1 8.7 copy-start.36
  446.1 8.7 copy-start.37
  446.1 8.7 copy-start.59
  446.1 8.7 copy-start.62
  446.1 8.7 copy-start.34
  446.1 8.7 copy-start.35
  446.1 8.7 copy-start.53
  446.1 8.7 copy-start.56
  466.5 56.7 %all-gather.13.cloned.1.call-start = ((), (), s32[]{:S(2)}) async-start(), calls=%async_computation.15 | async-start | bytes 1216512 | tf_op jit(solution)/shard_map/while/body/eval_jaxpr/all_gather | solution.py:291
  467.2 111.8 %all-gather.11.cloned.1.call-start = ((), (), s32[]{:S(2)}) async-start(), calls=%async_computation.14 | async-start | bytes 1216512 | tf_op jit(solution)/shard_map/while/body/eval_jaxpr/all_gather | solution.py:289
  467.9 167.0 %all-gather.7.cloned.1.call-start = ((), (), s32[]{:S(2)}) async-start(), calls=%async_computation.12 | async-start | bytes 1216512 | tf_op jit(solution)/shard_map/while/body/eval_jaxpr/all_gather | solution.py:288
  468.7 222.0 %all-gather.9.cloned.1.call-start = ((), (), s32[]{:S(2)}) async-start(), calls=%async_computation.13 | async-start | bytes 1216512 | tf_op jit(solution)/shard_map/while/body/eval_jaxpr/all_gather | solution.py:286
  469.3 286.9 %all-gather.15.cloned.1.call-start = ((), (), s32[]{:S(2)}) async-start(), calls=%async_computation.16 | async-start | bytes 4866048 | tf_op jit(solution)/shard_map/while/body/eval_jaxpr/all_gather | solution.py:297
  470.0 351.4 %all-gather.17.cloned.1.call-start = ((), (), s32[]{:S(2)}) async-start(), calls=%async_computation.17 | async-start | bytes 4866048 | tf_op jit(solution)/shard_map/while/body/eval_jaxpr/all_gather | solution.py:295
  856.0 11.3 copy-start.43
  856.0 11.3 copy-start.45
  856.0 11.3 copy-start.71
  856.0 11.3 copy-start.74
  856.0 11.4 copy-start.38
  856.0 11.4 copy-start.41
  856.0 11.4 copy-start.65
  856.0 11.4 copy-start.68
  856.0 11.4 copy-start.36
  856.0 11.4 copy-start.37
  856.0 11.4 copy-start.59
  856.0 11.4 copy-start.62
  856.1 11.4 copy-start.34
  856.1 11.4 copy-start.35
  856.1 11.4 copy-start.53
  856.1 11.4 copy-start.56
  880.5 151.5 %reduce-scatter.7.cloned.1.call-start = ((), (), s32[]{:S(2)}) async-start(), calls=%async_computation.6 | async-start | bytes 2433024 | tf_op jit(solution)/shard_map/reduce_scatter | solution.py:334
  881.0 255.5 %reduce-scatter.9.cloned.1.call-start = ((), (), s32[]{:S(2)}) async-start(), calls=%async_computation.7 | async-start | bytes 2433024 | tf_op jit(solution)/shard_map/reduce_scatter | solution.py:336
  881.6 358.6 %reduce-scatter.11.cloned.1.call-start = ((), (), s32[]{:S(2)}) async-start(), calls=%async_computation.8 | async-start | bytes 2433024 | tf_op jit(solution)/shard_map/reduce_scatter | solution.py:337
  882.2 462.8 %reduce-scatter.13.cloned.1.call-start = ((), (), s32[]{:S(2)}) async-start(), calls=%async_computation.9 | async-start | bytes 2433024 | tf_op jit(solution)/shard_map/reduce_scatter | solution.py:339
  883.0 603.2 %reduce-scatter.15.cloned.1.call-start = ((), (), s32[]{:S(2)}) async-start(), calls=%async_computation.10 | async-start | bytes 9732096 | tf_op jit(solution)/shard_map/reduce_scatter | solution.py:343
  883.7 744.5 %reduce-scatter.17.cloned.1.call-start = ((), (), s32[]{:S(2)}) async-start(), calls=%async_computation.11 | async-start | bytes 9732096 | tf_op jit(solution)/shard_map/reduce_scatter | solution.py:345
  (80 other events, 286.4 us)
Sparse Core Ops, SparseCore 0:
  12.4 56.8 all-gather.12
  72.2 52.9 all-gather.10
  128.1 52.9 all-gather.6
  183.8 52.9 all-gather.8
  239.6 62.5 all-gather.14
  304.9 62.4 all-gather.16
  470.2 52.8 all-gather.12
  526.0 52.9 all-gather.10
  581.9 52.9 all-gather.6
  637.7 52.9 all-gather.8
  693.6 62.5 all-gather.14
  759.0 62.4 all-gather.16
Sparse Core Ops, SparseCore 1:
  886.8 145.2 reduce-scatter.6
  1038.6 97.9 reduce-scatter.8
  1142.3 97.9 reduce-scatter.10
  1247.0 98.0 reduce-scatter.12
  1351.5 134.6 reduce-scatter.14
  1493.6 134.5 reduce-scatter.16
where the time goes:
time: 1640 us
  waiting for transfers between devices  1260 us (77%)
  blocking collectives  171 us (10%)
  other arithmetic  68.6 us (4%)
  local copies, waits for them, and re-layouts  60 us (4%)
  matrix products  53.2 us (3%)
    reduce_scatter x1, waiting for transfers between devices, on_device(): lax.psum_scatter(sum_w_fc2, 'fsdp', scatter_dimension=0, tiled=True)  142 us
    reduce_scatter x1, waiting for transfers between devices, on_device(): lax.psum_scatter(sum_w_fc1, 'fsdp', scatter_dimension=0, tiled=True)  141 us
    all_gather x2, waiting for transfers between devices, per_slot(): lax.all_gather(w_fc2, 'fsdp', axis=0, tiled=True)  131 us
    all_gather x2, waiting for transfers between devices, per_slot(): lax.all_gather(w_fc1, 'fsdp', axis=0, tiled=True)  130 us
    all_gather x2, waiting for transfers between devices, per_slot(): lax.all_gather(w_key, 'fsdp', axis=0, tiled=True)  112 us
    all_gather x2, waiting for transfers between devices, per_slot(): lax.all_gather(w_value, 'fsdp', axis=0, tiled=True)  112 us
    all_gather x2, waiting for transfers between devices, per_slot(): lax.all_gather(w_query, 'fsdp', axis=0, tiled=True)  111 us
    reduce_scatter x1, waiting for transfers between devices, on_device(): lax.psum_scatter(sum_w_out, 'fsdp', scatter_dimension=0, tiled=True)  105 us
  transfers between devices with their start and end apart: 18, of which 18 were waited for; matrix products, arithmetic and copies ran while one was open for 2% of the time, Pallas kernels for 0%

commit v1 on v0

v1 whole, which is shorter than its diff:
```python
import jax
import jax.numpy as jnp
from jax import lax
from jax.experimental import pallas as pl
from jax.experimental.pallas import tpu as pltpu
from jax.sharding import PartitionSpec as P

HD = 64
LENGTH = 128


EPS = 1e-05
BF = jnp.bfloat16
FL = jnp.float32


def normalize(values, gain, shift):
    center = values - jnp.mean(values, -1, keepdims=True)
    spread = jnp.mean(center * center, -1, keepdims=True)
    inverse = lax.rsqrt(spread + EPS)
    plain = center * inverse
    return (plain * gain.astype(FL) + shift.astype(FL), plain, inverse)


def norm_back(grad, plain, inverse, gain):
    scaled = grad * gain.astype(FL)
    inner = (
        scaled
        - jnp.mean(scaled, -1, keepdims=True)
        - plain * jnp.mean(scaled * plain, -1, keepdims=True)
    )
    return (inverse * inner, jnp.sum(grad * plain, 0), jnp.sum(grad, 0))


def project(left, right):
    return jnp.dot(left, right, preferred_element_type=FL)


def back_project(grad, right):
    return jnp.einsum("te,de->td", grad, right, preferred_element_type=FL)


def outer_sum(left, grad):
    return jnp.einsum("td,te->de", left, grad, preferred_element_type=FL)


MESH = pl.DeviceIdType.MESH
LANES = 128
VMEM_BYTES = 50 * 1024 * 1024
OFFSETS = (0, -1, 1, -2, 2, -3, 3)


def place():
    me = lax.axis_index("fsdp")
    z = me // 8
    core = me % 2
    across_x = 2 * (1 - 2 * ((me // 2) % 2))
    across_y = 4 * (1 - 2 * ((me // 4) % 2))
    first = across_x * (1 - core) + across_y * core
    second = across_x * core + across_y * (1 - core)
    return me, z, first, second, 1 - 2 * core


def greet(me, z, first, second, sibling):
    barrier = pltpu.get_barrier_semaphore()

    def signal(device):
        pl.semaphore_signal(barrier, inc=1, device_id=(device,), device_id_type=MESH)

    signal(me + first)
    signal(me + second)
    signal(me + sibling)

    @pl.when(z > 0)
    def _():
        signal(me - 8)

    @pl.when(z < 3)
    def _():
        signal(me + 8)

    pl.semaphore_wait(barrier, 3 + (z + 3) // 4 + (6 - z) // 4)


def gather_kernel(a_ref, b_ref, all_a, all_b, sent, landed, kept):
    me, z, first, second, sibling = place()
    ring = me % 8
    pairs = ((a_ref, all_a), (b_ref, all_b))
    locals_ = [
        pltpu.make_async_copy(own, whole.at[me], kept.at[k]) for k, (own, whole) in enumerate(pairs)
    ]
    for copy in locals_:
        copy.start()
    greet(me, z, first, second, sibling)

    def copies(block, device, slot, own=False):
        return [
            pltpu.make_async_remote_copy(
                src_ref=piece if own else whole.at[block],
                dst_ref=whole.at[block],
                send_sem=sent.at[k, slot],
                recv_sem=landed.at[k, block],
                device_id=(device,),
                device_id_type=MESH,
            )
            for k, (piece, whole) in enumerate(pairs)
        ]

    def send(block, device, slot, own=False):
        for copy in copies(block, device, slot, own):
            copy.start()

    def arrive(block):
        for copy in copies(block, me, 0):
            copy.wait_recv()

    def line(step, offset, finish):
        other = z + offset
        block = me + 8 * offset
        own = offset == 0

        def act(device, slot):
            if finish:
                for copy in copies(block, device, slot, own):
                    copy.wait_send()
            else:
                send(block, device, slot, own)

        @pl.when((other >= 0) & (other <= 3))
        def _():
            if not own and not finish:
                arrive(block)
            if offset <= 0:

                @pl.when(z < 3)
                def _():
                    act(me + 8, 4 * step)

            if offset >= 0:

                @pl.when(z > 0)
                def _():
                    act(me - 8, 4 * step + 3)

            act(me + first, 4 * step + 1)
            act(me + second, 4 * step + 2)
            act(me + sibling, 28 + step)

    def across(step, offset, near, far, finish):
        other = z + offset
        block = me + 8 * offset + near * first + far * second
        base = 35 + 7 * (near + 2 * far - 1)

        @pl.when((other >= 0) & (other <= 3))
        def _():
            if not finish:
                arrive(block)
                send(block, me + sibling, base + step)
                if not far:
                    send(block, me + second, 56 + step)
            else:
                for copy in copies(block, me + sibling, base + step):
                    copy.wait_send()
                if not far:
                    for copy in copies(block, me + second, 56 + step):
                        copy.wait_send()

    for finish in (False, True):
        for step in range(len(OFFSETS) + 2):
            if step < len(OFFSETS):
                line(step, OFFSETS[step], finish)
            if 1 <= step <= len(OFFSETS):
                across(step - 1, OFFSETS[step - 1], 1, 0, finish)
                across(step - 1, OFFSETS[step - 1], 0, 1, finish)
            if step >= 2:
                across(step - 2, OFFSETS[step - 2], 1, 1, finish)
    for index in range(16):
        arrive(2 * index + (ring + sibling) % 2)
    for copy in locals_:
        copy.wait()


def gather_blocks(a, b, devices):
    if devices != 32:
        return lax.all_gather(a, "fsdp", axis=0), lax.all_gather(b, "fsdp", axis=0)
    return pl.pallas_call(
        gather_kernel,
        out_shape=(
            jax.ShapeDtypeStruct((devices,) + a.shape, a.dtype),
            jax.ShapeDtypeStruct((devices,) + b.shape, b.dtype),
        ),
        in_specs=[pl.BlockSpec(memory_space=pl.ANY)] * 2,
        out_specs=(pl.BlockSpec(memory_space=pl.ANY),) * 2,
        scratch_shapes=[
            pltpu.SemaphoreType.DMA((2, 64)),
            pltpu.SemaphoreType.DMA((2, 32)),
            pltpu.SemaphoreType.DMA((2,)),
        ],
        compiler_params=pltpu.CompilerParams(
            collective_id=0, has_side_effects=True, vmem_limit_bytes=VMEM_BYTES
        ),
    )(a, b)


def scatter_kernel(
    a_ref,
    b_ref,
    out_a,
    out_b,
    own_a,
    own_b,
    pair_a,
    pair_b,
    two_a,
    two_b,
    one_a,
    one_b,
    line_a,
    line_b,
    sent,
    landed,
    loaded,
):
    me, z, first, second, sibling = place()
    ring = me % 8
    whole = (a_ref, b_ref)
    own, pair = (own_a, own_b), (pair_a, pair_b)
    two, one, lane = (two_a, two_b), (one_a, one_b), (line_a, line_b)
    final = (out_a, out_b)

    def slot16(block):
        return block // 2

    def targets():
        for a, b in ((1, 1), (0, 1), (1, 0), (0, 0)):
            for to in range(4):
                yield to, a, b

    loads = []
    for order, (to, a, b) in enumerate(targets()):
        block = 8 * to + ring + a * first + b * second
        for k in range(2):
            copy = pltpu.make_async_copy(
                whole[k].at[block], own[k].at[slot16(block)], loaded.at[k, order]
            )
            copy.start()
            loads.append(copy)
    greet(me, z, first, second, sibling)

    def remote(source, target, k, out_slot, in_slot, device):
        return pltpu.make_async_remote_copy(
            src_ref=source,
            dst_ref=target,
            send_sem=sent.at[k, out_slot],
            recv_sem=landed.at[k, in_slot],
            device_id=(device,),
            device_id_type=MESH,
        )

    def pair_copy(order, to, a, b, k):
        block = 8 * to + (ring + sibling) + b * first + a * second
        return remote(
            whole[k].at[block], pair[k].at[slot16(block)], k, order, slot16(block), me + sibling
        )

    for order, (to, a, b) in enumerate(targets()):
        for k in range(2):
            pair_copy(order, to, a, b, k).start()

    def add(k, target, sources):
        if k == 0:
            wide = target.shape[-1]
            chunk = LANES * max(d for d in range(1, 9) if (wide // LANES) % d == 0)

            @pl.loop(0, wide // chunk)
            def _(i):
                part = pl.ds(pl.multiple_of(i * chunk, LANES), chunk)
                total = sources[0][:, part].astype(FL)
                for source in sources[1:]:
                    total = total + source[:, part].astype(FL)
                target[:, part] = total.astype(target.dtype)
        else:
            chunk = 16

            @pl.loop(0, target.shape[0] // chunk)
            def _(i):
                part = pl.ds(pl.multiple_of(i * chunk, chunk), chunk)
                total = sources[0][part, :].astype(FL)
                for source in sources[1:]:
                    total = total + source[part, :].astype(FL)
                target[part, :] = total.astype(target.dtype)

    def base(order, to, a, b, k):
        block = 8 * to + ring + a * first + b * second
        slot = slot16(block)
        loads[2 * order + k].wait()
        remote(whole[k].at[block], pair[k].at[slot], k, 0, slot, me).wait_recv()
        return own[k].at[slot], pair[k].at[slot]

    def second_copy(to, a, k, source):
        return remote(source, two[k].at[2 * to + a], k, 16 + 2 * to + a, 16 + 2 * to + a, me + second)

    def first_copy(to, k, source):
        return remote(source, one[k].at[to], k, 24 + to, 24 + to, me + first)

    orders = list(targets())
    for order, (to, a, b) in enumerate(orders[:8]):
        for k in range(2):
            mine, theirs = base(order, to, a, b, k)
            add(k, mine, (mine, theirs))
            second_copy(to, a, k, mine).start()
    for order in range(8, 12):
        to, a, b = orders[order]
        for k in range(2):
            mine, theirs = base(order, to, a, b, k)
            second_copy(to, a, k, mine).wait_recv()
            add(k, mine, (mine, theirs, two[k].at[2 * to + a]))
            first_copy(to, k, mine).start()
    for order in range(12, 16):
        to, a, b = orders[order]
        for k in range(2):
            mine, theirs = base(order, to, a, b, k)
            second_copy(to, a, k, mine).wait_recv()
            first_copy(to, k, mine).wait_recv()
            add(k, mine, (mine, theirs, two[k].at[2 * to + a], one[k].at[to]))

    def along(goal, k, upward):
        slot = 28 + goal + (0 if upward else 4)
        place_in = goal + (0 if upward else 4)
        mine = own[k].at[slot16(8 * goal + ring)]
        return mine, remote(
            mine, lane[k].at[place_in], k, slot, slot, me + 8 if upward else me - 8
        )

    for goal in (3, 2, 1):
        for k in range(2):
            mine, copy = along(goal, k, True)

            @pl.when(z < goal)
            def _():
                @pl.when(z > 0)
                def _():
                    copy.wait_recv()
                    add(k, mine, (mine, lane[k].at[goal]))

                copy.start()

            down = 3 - goal
            mine_down, copy_down = along(down, k, False)

            @pl.when(z > down)
            def _():
                @pl.when(z < 3)
                def _():
                    copy_down.wait_recv()
                    add(k, mine_down, (mine_down, lane[k].at[4 + down]))

                copy_down.start()

    for goal in range(4):

        @pl.when(z == goal)
        def _():
            for k in range(2):
                mine = own[k].at[slot16(8 * goal + ring)]
                sources = [mine]
                if goal > 0:
                    along(goal, k, True)[1].wait_recv()
                    sources.append(lane[k].at[goal])
                if goal < 3:
                    along(goal, k, False)[1].wait_recv()
                    sources.append(lane[k].at[4 + goal])
                add(k, final[k], sources)

    for order, (to, a, b) in enumerate(orders):
        for k in range(2):
            pair_copy(order, to, a, b, k).wait_send()
            mine = own[k].at[0]
            if order < 8:
                second_copy(to, a, k, mine).wait_send()
            elif order < 12:
                first_copy(to, k, mine).wait_send()
    for goal in range(4):
        for k in range(2):

            @pl.when(z < goal)
            def _():
                along(goal, k, True)[1].wait_send()

            @pl.when(z > goal)
            def _():
                along(goal, k, False)[1].wait_send()


def scatter_blocks(a, b, devices):
    if devices != 32:
        return (
            lax.psum_scatter(a.astype(FL), "fsdp", scatter_dimension=0),
            lax.psum_scatter(b.astype(FL), "fsdp", scatter_dimension=0),
        )
    vmem = pl.BlockSpec(memory_space=pltpu.VMEM)
    scratch = []
    for count in (16, 16, 8, 4, 8):
        scratch.append(pltpu.VMEM((count,) + a.shape[1:], BF))
        scratch.append(pltpu.VMEM((count,) + b.shape[1:], BF))
    return pl.pallas_call(
        scatter_kernel,
        out_shape=(
            jax.ShapeDtypeStruct(a.shape[1:], FL),
            jax.ShapeDtypeStruct(b.shape[1:], FL),
        ),
        in_specs=[pl.BlockSpec(memory_space=pl.ANY)] * 2,
        out_specs=(vmem, vmem),
        scratch_shapes=scratch
        + [
            pltpu.SemaphoreType.DMA((2, 36)),
            pltpu.SemaphoreType.DMA((2, 36)),
            pltpu.SemaphoreType.DMA((2, 16)),
        ],
        compiler_params=pltpu.CompilerParams(
            collective_id=1, has_side_effects=True, vmem_limit_bytes=VMEM_BYTES
        ),
    )(a, b)


def column_sums(values):
    return jnp.sum(values, 0)


def on_device(
    tokens,
    cotangent,
    counts,
    ln1_gain,
    ln1_bias,
    w_query,
    b_query,
    w_key,
    w_value,
    b_value,
    w_out,
    b_out,
    ln2_gain,
    ln2_bias,
    w_fc1,
    b_fc1,
    w_fc2,
    b_fc2,
):
    devices = lax.axis_size("fsdp")
    rows, width = tokens.shape
    slots = rows // LENGTH
    heads = width // HD
    depth = w_query.shape[0]
    hidden = w_fc1.shape[1]
    wide = 4 * width + hidden

    vectors = (ln1_gain, ln1_bias, b_query, b_value, b_out, ln2_gain, ln2_bias, b_fc2)
    few = len(vectors)
    per_row = b_fc1.shape[0] // depth
    small = jnp.concatenate(
        [jnp.stack(vectors, 1), b_fc1.reshape(depth, per_row)], axis=1
    )
    small = jnp.pad(small, ((0, 0), (0, LANES - small.shape[1])))
    block_a = jnp.concatenate([w_query, w_key, w_value, w_out, w_fc1, small], axis=1)
    all_a, all_b = gather_blocks(block_a, w_fc2, devices)
    all_a = all_a.reshape(width, wide + LANES)
    w_in = all_a[:, : 3 * width]
    w_out = all_a[:, 3 * width : 4 * width]
    w_fc1 = all_a[:, 4 * width : wide]
    w_fc2 = all_b.reshape(hidden, width)
    small = all_a[:, wide : wide + few + per_row].astype(FL)
    ln1_gain, ln1_bias, b_query, b_value, b_out, ln2_gain, ln2_bias, b_fc2 = small[:, :few].T
    b_fc1 = small[:, few:].reshape(hidden)

    live = (jnp.arange(rows, dtype=jnp.int32) // LENGTH < counts[0]).astype(FL)[:, None]
    inputs = tokens.astype(FL)
    normed_full, plain_one, inverse_one = normalize(inputs, ln1_gain, ln1_bias)
    normed = normed_full.astype(BF)
    b_in = jnp.concatenate([b_query, jnp.zeros_like(b_query), b_value])
    in_rows = (project(normed, w_in) + b_in).astype(BF)

    def split(values):
        return values.reshape(slots, LENGTH, heads, HD)

    queries = split(in_rows[:, :width])
    key_rows = split(in_rows[:, width : 2 * width])
    value_rows = split(in_rows[:, 2 * width :])
    scores = jnp.einsum("bqhd,bkhd->bhqk", queries, key_rows, preferred_element_type=FL)
    scores = scores * HD ** (-0.5)
    causal = jnp.arange(LENGTH)[:, None] >= jnp.arange(LENGTH)[None, :]
    scores = jnp.where(causal, scores, -1e30)
    highest = jnp.max(scores, -1, keepdims=True)
    expo = jnp.exp(scores - highest)
    probs = expo / jnp.sum(expo, -1, keepdims=True)
    weights = probs.astype(BF)
    attended = jnp.einsum("bhqk,bkhd->bqhd", weights, value_rows, preferred_element_type=FL)
    attended = attended.reshape(rows, width).astype(BF)
    middle = inputs + project(attended, w_out) + b_out
    normed_two_full, plain_two, inverse_two = normalize(middle, ln2_gain, ln2_bias)
    normed_two = normed_two_full.astype(BF)
    hidden_pre = project(normed_two, w_fc1) + b_fc1
    gelu, gelu_pull = jax.vjp(jax.nn.gelu, hidden_pre)
    activated = gelu.astype(BF)
    mixed = (live * (middle + project(activated, w_fc2) + b_fc2)).astype(BF)

    grad_out = cotangent.astype(FL) * live
    grad_rows = grad_out.astype(BF)
    grad_w_fc2 = outer_sum(activated, grad_rows)
    grad_act = back_project(grad_rows, w_fc2)
    grad_pre = gelu_pull(grad_act)[0].astype(BF)
    grad_w_fc1 = outer_sum(normed_two, grad_pre)
    grad_norm_two = back_project(grad_pre, w_fc1)
    through_two, grad_ln2_gain, grad_ln2_bias = norm_back(
        grad_norm_two, plain_two, inverse_two, ln2_gain
    )
    grad_middle = grad_out + through_two
    grad_branch = grad_middle.astype(BF)
    grad_w_out = outer_sum(attended, grad_branch)
    grad_att = split(back_project(grad_branch, w_out).astype(BF))
    grad_probs = jnp.einsum("bqhd,bkhd->bhqk", grad_att, value_rows, preferred_element_type=FL)
    grad_values = jnp.einsum("bhqk,bqhd->bkhd", weights, grad_att, preferred_element_type=FL)
    grad_scores = probs * (grad_probs - jnp.sum(probs * grad_probs, -1, keepdims=True))
    grad_scores = grad_scores.astype(BF)
    grad_queries = jnp.einsum("bhqk,bkhd->bqhd", grad_scores, key_rows, preferred_element_type=FL)
    grad_keys = jnp.einsum("bhqk,bqhd->bkhd", grad_scores, queries, preferred_element_type=FL)
    grad_in = jnp.concatenate(
        [
            (grad_queries * HD ** (-0.5)).astype(BF).reshape(rows, width),
            (grad_keys * HD ** (-0.5)).astype(BF).reshape(rows, width),
            grad_values.astype(BF).reshape(rows, width),
        ],
        axis=1,
    )
    grad_w_in = outer_sum(normed, grad_in)
    grad_norm_one = back_project(grad_in, w_in)
    through_one, grad_ln1_gain, grad_ln1_bias = norm_back(
        grad_norm_one, plain_one, inverse_one, ln1_gain
    )
    grad_tokens = grad_middle + through_one

    in_sums = column_sums(grad_in.astype(FL))
    vectors = (
        grad_ln1_gain,
        grad_ln1_bias,
        in_sums[:width],
        in_sums[2 * width :],
        column_sums(grad_branch.astype(FL)),
        grad_ln2_gain,
        grad_ln2_bias,
        column_sums(grad_out),
    )
    small = jnp.concatenate(
        [jnp.stack(vectors, 1), column_sums(grad_pre.astype(FL)).reshape(width, per_row)], axis=1
    )
    small = jnp.pad(small, ((0, 0), (0, LANES - small.shape[1])))
    sums_a = jnp.concatenate(
        [grad_w_in.astype(BF), grad_w_out.astype(BF), grad_w_fc1.astype(BF), small.astype(BF)],
        axis=1,
    )
    got_a, got_b = scatter_blocks(
        sums_a.reshape(devices, depth, wide + LANES),
        grad_w_fc2.astype(BF).reshape((devices,) + (hidden // devices, width)),
        devices,
    )
    small = got_a[:, wide : wide + few + per_row]
    columns = tuple(small[:, i] for i in range(few))
    return (
        mixed,
        grad_tokens,
        columns[0],
        columns[1],
        got_a[:, :width],
        columns[2],
        got_a[:, width : 2 * width],
        got_a[:, 2 * width : 3 * width],
        columns[3],
        got_a[:, 3 * width : 4 * width],
        columns[4],
        columns[5],
        columns[6],
        got_a[:, 4 * width : wide],
        small[:, few:].reshape(hidden // devices),
        got_b,
        columns[7],
    )


def solution(mesh):
    in_specs = (
        P("fsdp", None),
        P("fsdp", None),
        P("fsdp"),
        P("fsdp"),
        P("fsdp"),
        P("fsdp", None),
        P("fsdp"),
        P("fsdp", None),
        P("fsdp", None),
        P("fsdp"),
        P("fsdp", None),
        P("fsdp"),
        P("fsdp"),
        P("fsdp"),
        P("fsdp", None),
        P("fsdp"),
        P("fsdp", None),
        P("fsdp"),
    )
    out_specs = (
        P("fsdp", None),
        P("fsdp", None),
        P("fsdp"),
        P("fsdp"),
        P("fsdp", None),
        P("fsdp"),
        P("fsdp", None),
        P("fsdp", None),
        P("fsdp"),
        P("fsdp", None),
        P("fsdp"),
        P("fsdp"),
        P("fsdp"),
        P("fsdp", None),
        P("fsdp"),
        P("fsdp", None),
        P("fsdp"),
    )
    return jax.shard_map(
        on_device, mesh=mesh, in_specs=in_specs, out_specs=out_specs, check_vma=False
    )
```

time: 1640 us -> 282 us (0.17)
  waiting for transfers between devices: 1260 us -> 0 us
  Pallas kernels: 0 us -> 182 us
  blocking collectives: 171 us -> 0 us
  other arithmetic: 68.6 us -> 14.2 us
  local copies, waits for them, and re-layouts: 60 us -> 39.3 us
    reduce_scatter x6 -> x0, waiting for transfers between devices: 650 us -> none  [the longest x1 142 us: on_device(): lax.psum_scatter(sum_w_fc2, 'fsdp', scatter_dimension=0, tiled=True)]
    all_gather x12 -> x0, waiting for transfers between devices: 601 us -> none  [the longest x2 131 us: per_slot(): lax.all_gather(w_fc2, 'fsdp', axis=0, tiled=True)]
    pallas_call x0 -> x2, Pallas kernels: none -> 182 us  [the longest x1 101 us: scatter_blocks(): pl.pallas_call(scatter_kernel, out_shape=(jax.ShapeDtypeStruct(a.shape[1:...]
    unnamed x1 -> x0, blocking collectives: 88.1 us -> none
    while x2 -> x0, blocking collectives: 82.6 us -> none
    add x18 -> x1, other arithmetic: 65.2 us -> 1.19 us  [on_device(): grad_tokens = grad_middle + through_one]
    while x160 -> x0, local copies, waits for them, and re-layouts: 19.6 us -> none
  transfers between devices with their start and end apart: 18 -> 0, of which waited for: 18 -> 0; matrix products, arithmetic and copies ran while one was open for 2% -> 0% of each run, Pallas kernels for 0% -> 0%
where the time goes in v1:
time: 282 us; the launch traced here: 280 us
  Pallas kernels  182 us (65%)
  matrix products  42.6 us (15%)
  local copies, waits for them, and re-layouts  39.3 us (14%)
  other arithmetic  14.2 us (5%)
    pallas_call x1, Pallas kernels, scatter_blocks(): pl.pallas_call(scatter_kernel, out_shape=(jax.ShapeDtypeStruct(a.shape[1:...  101 us
    pallas_call x1, Pallas kernels, gather_blocks(): pl.pallas_call(gather_kernel, out_shape=(jax.ShapeDtypeStruct((devices,)...  80.3 us
    another operation x16, local copies, waits for them, and re-layouts, on_device(): jnp.stack(vectors, 1)  14.8 us
    dot_general x4, matrix products, outer_sum(): return jnp.einsum('td,te->de', left, grad, preferred_element_type=FL)  12.5 us
    dot_general x4, matrix products, project(): return jnp.dot(left, right, preferred_element_type=FL)  11.8 us
    dot_general x4, matrix products, back_project(): return jnp.einsum('te,de->td', grad, right, preferred_element_type=FL)  10.9 us
    unnamed x85, local copies, waits for them, and re-layouts  8.35 us
    concatenate x1, other arithmetic, on_device(): jnp.concatenate([grad_w_in.astype(BF), grad_w_out.astype(BF), grad_w_fc1....  6.85 us

profile of v1, /device:TPU:0, one launch (start us, length us, event | category | flops | bytes accessed | tf_op | source)
XLA Modules:
  0.0 279.8 jit_solution(6731773441489803134)
XLA Ops:
  0.7 0.8 constant_dynamic-update-slice_fusion.5
  1.4 0.8 constant_dynamic-update-slice_fusion.4
  2.2 0.8 constant_dynamic-update-slice_fusion.3
  3.0 0.8 constant_dynamic-update-slice_fusion.2
  3.7 0.9 constant_dynamic-update-slice_fusion.1
  4.7 0.7 copy.128
  5.4 0.7 copy.129
  6.2 0.7 copy.130
  6.9 0.7 copy.131
  10.6 0.7 reshape.139
  11.5 0.9 copy-done
  12.4 80.3 %shard_map.305 = (bf16[32,24,6272]{2,1,0:T(8,128)(2,1)}, bf16[32,96,768]{2,1,0:T(8,128)(2,1)}) custom-call(bf16[24,6272]{1,0:T(8,128)(2,1)S(1)} %constant_dynamic-update-slice_fusion.a_ref, bf16[96,768]{1,0:T(8,128)(2,1)S(1)} %copy-done), custom_call_target="tpu_custom_call" | custom-call | tf_op jit(solution)/shard_map/pallas_call | solution.py:186
  92.8 0.9 slice.112
  94.5 1.1 convert_reduce_fusion
  95.7 1.2 fusion.48
  97.5 3.3 %fusion.10 = bf16[256,2304]{1,0:T(8,128)(2,1)S(1)} fusion(bf16[768,6272]{1,0:T(8,128)(2,1)} %bitcast.79, f32[2304]{0:T(1024)S(1)} %pad_maximum_fusion, bf16[256,768]{1,0:T(8,128)(2,1)} %param.18, f32[768]{0:T(1024)S(1)} %get-tuple-element.47, f32[768]{0:T(1024)S(1)} %get-tuple-element.48, f32[256]{0:T(256)S(1)} %add_rsqrt_fusion.1, ...), kind=kOutput, calls=%fused_computation.15 | convolution fusion | flops 908328960 | bytes 5129216 | tf_op jit(solution)/shard_map/dot_general | solution.py:36
  101.7 1.8 fusion.89
  104.2 1.8 fusion.31
  106.4 1.9 fusion.94
  109.7 4.0 %fusion.7 = f32[256,3072]{1,0:T(8,128)S(1)} fusion(bf16[768,6272]{1,0:T(8,128)(2,1)} %bitcast.81, f32[3072]{0:T(1024)S(1)} %add.116, f32[256,768]{1,0:T(8,128)S(1)} %get-tuple-element.63, f32[768]{0:T(1024)S(1)} %get-tuple-element.43, f32[768]{0:T(1024)S(1)} %get-tuple-element.41, f32[256]{0:T(256)S(1)} %add_rsqrt_fusion, f32[256]{0:T(256)S(1)} %broadcast_multiply_fusion.4), kind=kOutput, calls=%fused_computation.14 | convolution fusion | flops 1209729024 | bytes 8671232 | tf_op jit(solution)/shard_map/dot_general | solution.py:36
  113.8 2.7 fusion.28
  116.5 4.9 %fusion.95 = (bf16[3072]{0:T(1024)(128)(2,1)}, bf16[256,3072]{1,0:T(8,128)(2,1)S(1)}) fusion(f32[256,3072]{1,0:T(8,128)S(1)} %fusion.7, bf16[3072,768]{1,0:T(8,128)(2,1)S(1)} %bitcast.98, bf16[256,768]{1,0:T(8,128)(2,1)S(1)} %copy-done.6, f32[256]{0:T(256)S(1)} %compare_convert_fusion), kind=kOutput, calls=%fused_computation.148 | convolution fusion | flops 1225061376 | bytes 9837568 | tf_op jit(solution)/shard_map/te,de->td/dot_general | solution.py:40
  121.4 2.1 multiply_reduce_fusion.1
  123.6 1.0 convert_reduce_fusion.1
  125.4 2.1 multiply_reduce_fusion
  131.0 3.4 %fusion.47 = (bf16[768]{0:T(1024)(128)(2,1)S(1)}, f32[256]{0:T(256)S(1)}, f32[256]{0:T(256)S(1)}, bf16[768]{0:T(1024)(128)(2,1)S(1)}, f32[256,768]{1,0:T(8,128)S(1)}) fusion(bf16[256,768]{1,0:T(8,128)(2,1)S(1)} %copy-done.1, f32[256]{0:T(256)S(1)} %copy-done.22, f32[256]{0:T(256)S(1)} %copy-done.16, f32[768]{0:T(1024)S(1)} %get-tuple-element.48, ...), kind=kOutput, calls=%fused_computation.66 | convolution fusion | flops 907933696 | bytes 5908480 | tf_op jit(solution)/shard_map/te,de->td/dot_general | solution.py:40
  134.4 1.2 fusion.46
  135.6 0.8 stack.72
  136.5 0.8 stack.73
  137.3 1.0 reduce
  139.0 0.9 stack.74
  139.8 0.8 stack.75
  140.7 1.5 stack.76
  142.2 1.5 stack.77
  143.7 1.5 stack.78
  145.2 1.2 fusion.49
  146.4 0.9 stack.79
  147.3 1.8 reshape.149
  149.1 2.5 concatenate.23
  151.6 5.1 %convolution_convert_fusion.1 = bf16[768,3072]{1,0:T(8,128)(2,1)} fusion(bf16[256,3072]{1,0:T(8,128)(2,1)} %copy-done.8, f32[256,768]{1,0:T(8,128)S(1)} %get-tuple-element.63, f32[768]{0:T(1024)S(1)} %get-tuple-element.43, f32[768]{0:T(1024)S(1)} %get-tuple-element.41, f32[256]{0:T(256)} %copy-done.24, f32[256]{0:T(256)} %copy-done.18), kind=kOutput, calls=%fused_computation.5 | convolution fusion | flops 1211301888 | bytes 7086080 | tf_op jit(solution)/shard_map/td,te->de/dot_general | solution.py:44
  156.7 1.5 convolution_convert_fusion.3
  158.3 2.4 copy.166
  160.8 1.3 convolution_convert_fusion.2
  162.1 0.8 slice-done.1
  163.3 6.8 %fusion.2 = bf16[768,6272]{1,0:T(8,128)(2,1)} fusion(bf16[768,12]{1,0:T(8,128)(2,1)S(1)} %copy-done.9, bf16[768,3072]{1,0:T(8,128)(2,1)S(1)} %bitcast.71, bf16[768,768]{1,0:T(8,128)(2,1)S(1)} %copy-done.2, bf16[768,2304]{1,0:T(8,128)(2,1)S(1)} %convolution_convert_fusion.2), kind=kLoop, calls=%fused_computation.3 | loop fusion | flops 48168960 | bytes 19089408 | tf_op jit(solution)/shard_map/concatenate | solution.py:557
  170.1 4.5 %convolution_convert_fusion = bf16[3072,768]{1,0:T(8,128)(2,1)} fusion(bf16[256,768]{1,0:T(8,128)(2,1)S(1)} %copy-done.7, f32[256]{0:T(256)S(1)} %copy-done.26, f32[256,3072]{1,0:T(8,128)S(1)} %copy-done.30), kind=kOutput, calls=%fused_computation.4 | convolution fusion | flops 1217986560 | bytes 8258560 | tf_op jit(solution)/shard_map/td,te->de/dot_general | solution.py:44
  174.7 101.5 %shard_map.306 = (f32[24,6272]{1,0:T(8,128)S(1)}, f32[96,768]{1,0:T(8,128)S(1)}) custom-call(bf16[32,24,6272]{2,1,0:T(8,128)(2,1)} %bitcast.69, bf16[32,96,768]{2,1,0:T(8,128)(2,1)} %bitcast.72), custom_call_target="tpu_custom_call" | custom-call | tf_op jit(solution)/shard_map/pallas_call | solution.py:406
  276.1 0.8 slice_reduce_fusion
  (129 shorter events, 15.2 us)
Async XLA Ops:
  11.5 0.9 copy-start
  93.8 3.1 %copy-start.13 = (bf16[768,12]{0,1:T(8,128)(2,1)}, bf16[768,12]{0,1:T(8,128)(2,1)S(1)}, u32[]{:S(2)}) copy-start(bf16[768,12]{0,1:T(8,128)(2,1)S(1)} %copy.171) | copy-start | bytes 55300
  95.7 1.3 copy-start.15
  96.9 0.5 copy-start.21
  101.1 2.4 copy-start.10
  101.7 4.2 %copy-start.3 = (bf16[2,128,12,64]{1,0,3,2:T(2,128)(2,1)}, bf16[2,128,12,64]{1,0,3,2:T(2,128)(2,1)S(1)}, u32[]{:S(2)}) copy-start(bf16[2,128,12,64]{1,0,3,2:T(2,128)(2,1)S(1)} %reshape.142) | copy-start | bytes 1179652
  103.6 0.6 copy-start.19
  104.2 2.3 copy-start.1
  104.2 2.3 copy-start.28
  106.0 3.0 %copy-start.14 = (bf16[768,12]{0,1:T(8,128)(2,1)S(1)}, bf16[768,12]{0,1:T(8,128)(2,1)}, u32[]{:S(2)}) copy-start(bf16[768,12]{0,1:T(8,128)(2,1)} %copy-done.13) | copy-start | bytes 55300
  109.0 14.6 %copy-start.25 = (f32[256]{0:T(256)}, f32[256]{0:T(256)S(1)}, u32[]{:S(2)}) copy-start(f32[256]{0:T(256)S(1)} %compare_convert_fusion) | copy-start | bytes 3076
  109.4 14.1 %copy-start.18 = (f32[256]{0:T(256)}, f32[256]{0:T(256)S(1)}, u32[]{:S(2)}) copy-start(f32[256]{0:T(256)S(1)} %broadcast_multiply_fusion.4) | copy-start | bytes 3076
  109.4 4.2 %slice-start.5 = ((s8[4718592]{0:T(1024)(128)(4,1)}), s8[4194304]{0:T(1024)(128)(4,1)S(1)}, s32[]{:S(2)}) async-start(s8[4718592]{0:T(1024)(128)(4,1)} %bitcast.95), calls=%async_computation.5 | async-start | bytes 8388608
  109.7 13.9 %copy-start.24 = (f32[256]{0:T(256)}, f32[256]{0:T(256)S(1)}, u32[]{:S(2)}) copy-start(f32[256]{0:T(256)S(1)} %add_rsqrt_fusion) | copy-start | bytes 3076
  109.7 4.0 %copy-start.27 = (f32[768]{0:T(1024)S(1)}, f32[768]{0:T(1024)}, u32[]{:S(2)}) copy-start(f32[768]{0:T(1024)} %get-tuple-element.42) | copy-start | bytes 9220
  109.7 4.0 %slice-start.6 = ((s8[4718592]{0:T(1024)(128)(4,1)}), s8[524288]{0:T(1024)(128)(4,1)S(1)}, s32[]{:S(2)}) async-start(s8[4718592]{0:T(1024)(128)(4,1)} %bitcast.95), calls=%async_computation.6 | async-start | bytes 1048576
  113.7 2.8 copy-start.29
  113.7 2.8 copy-start.6
  113.7 7.7 %slice-start.2 = ((s8[9633792]{0:T(1024)(128)(4,1)}), s8[4194304]{0:T(1024)(128)(4,1)S(1)}, s32[]{:S(2)}) async-start(s8[9633792]{0:T(1024)(128)(4,1)} %bitcast.83), calls=%async_computation.2 | async-start | bytes 8388608
  113.7 7.6 %slice-start.3 = ((s8[9633792]{0:T(1024)(128)(4,1)}), s8[4194304]{0:T(1024)(128)(4,1)S(1)}, s32[]{:S(2)}) async-start(s8[9633792]{0:T(1024)(128)(4,1)} %bitcast.83), calls=%async_computation.3 | async-start | bytes 8388608
  116.5 4.9 %slice-start.4 = ((s8[9633792]{0:T(1024)(128)(4,1)}), s8[1245184]{0:T(1024)(128)(4,1)S(1)}, s32[]{:S(2)}) async-start(s8[9633792]{0:T(1024)(128)(4,1)} %bitcast.83), calls=%async_computation.4 | async-start | bytes 2490368
  121.4 3.1 %copy-start.8 = (bf16[256,3072]{1,0:T(8,128)(2,1)}, bf16[256,3072]{1,0:T(8,128)(2,1)S(1)}, u32[]{:S(2)}) copy-start(bf16[256,3072]{1,0:T(8,128)(2,1)S(1)} %get-tuple-element.69) | copy-start | bytes 4718596
  125.3 2.1 copy-start.11
  125.3 2.2 copy-start.5
  125.3 2.1 copy-start.20
  127.5 1.2 copy-start.4
  127.9 2.0 copy-start.12
  129.8 1.2 copy-start.16
  129.9 1.2 copy-start.22
  156.7 4.0 %copy-start.17 = (f32[256]{0:T(256)S(1)}, f32[256]{0:T(256)}, u32[]{:S(2)}) copy-start(f32[256]{0:T(256)} %copy-done.15) | copy-start | bytes 3076
  156.7 4.0 %copy-start.23 = (f32[256]{0:T(256)S(1)}, f32[256]{0:T(256)}, u32[]{:S(2)}) copy-start(f32[256]{0:T(256)} %copy-done.21) | copy-start | bytes 3076
  158.3 3.8 %slice-start = ((s8[4718592]{0:T(1024)(128)(4,1)}), s8[524288]{0:T(1024)(128)(4,1)S(1)}, s32[]{:S(2)}) async-start(s8[4718592]{0:T(1024)(128)(4,1)} %bitcast.70), calls=%async_computation | async-start | bytes 1048576
  160.7 2.2 slice-start.1
  160.7 2.5 copy-start.2
  160.7 2.5 copy-start.9
  163.3 6.9 %copy-start.7 = (bf16[256,768]{1,0:T(8,128)(2,1)S(1)}, bf16[256,768]{1,0:T(8,128)(2,1)}, u32[]{:S(2)}) copy-start(bf16[256,768]{1,0:T(8,128)(2,1)} %param.19) | copy-start | bytes 1179652
  163.3 6.9 %copy-start.26 = (f32[256]{0:T(256)S(1)}, f32[256]{0:T(256)}, u32[]{:S(2)}) copy-start(f32[256]{0:T(256)} %copy-done.25) | copy-start | bytes 3076
  163.3 6.9 %copy-start.30 = (f32[256,3072]{1,0:T(8,128)S(1)}, f32[256,3072]{1,0:T(8,128)}, u32[]{:S(2)}) copy-start(f32[256,3072]{1,0:T(8,128)} %copy-done.29) | copy-start | bytes 9437188

commit v2 on v1

--- a/solution.py
+++ b/solution.py
@@ -93,7 +93,7 @@
         copy.start()
     greet(me, z, first, second, sibling)
 
-    def copies(block, device, slot, own=False):
+    def copies(block, device, slot, own=False, only=(0, 1)):
         return [
             pltpu.make_async_remote_copy(
                 src_ref=piece if own else whole.at[block],
@@ -104,14 +104,15 @@
                 device_id_type=MESH,
             )
             for k, (piece, whole) in enumerate(pairs)
+            if k in only
         ]
 
-    def send(block, device, slot, own=False):
-        for copy in copies(block, device, slot, own):
+    def send(block, device, slot, own=False, only=(0, 1)):
+        for copy in copies(block, device, slot, own, only):
             copy.start()
 
-    def arrive(block):
-        for copy in copies(block, me, 0):
+    def arrive(block, only=(0, 1)):
+        for copy in copies(block, me, 0, only=only):
             copy.wait_recv()
 
     def line(step, offset, finish):
@@ -119,32 +120,33 @@
         block = me + 8 * offset
         own = offset == 0
 
-        def act(device, slot):
+        def act(device, slot, k):
             if finish:
-                for copy in copies(block, device, slot, own):
+                for copy in copies(block, device, slot, own, (k,)):
                     copy.wait_send()
             else:
-                send(block, device, slot, own)
+                send(block, device, slot, own, (k,))
 
         @pl.when((other >= 0) & (other <= 3))
         def _():
-            if not own and not finish:
-                arrive(block)
-            if offset <= 0:
-
-                @pl.when(z < 3)
-                def _():
-                    act(me + 8, 4 * step)
-
-            if offset >= 0:
-
-                @pl.when(z > 0)
-                def _():
-                    act(me - 8, 4 * step + 3)
-
-            act(me + first, 4 * step + 1)
-            act(me + second, 4 * step + 2)
-            act(me + sibling, 28 + step)
+            for k in range(2):
+                if not own and not finish:
+                    arrive(block, (k,))
+                if offset <= 0:
+
+                    @pl.when(z < 3)
+                    def _():
+                        act(me + 8, 4 * step, k)
+
+                if offset >= 0:
+
+                    @pl.when(z > 0)
+                    def _():
+                        act(me - 8, 4 * step + 3, k)
+
+                act(me + first, 4 * step + 1, k)
+                act(me + second, 4 * step + 2, k)
+                act(me + sibling, 28 + step, k)
 
     def across(step, offset, near, far, finish):
         other = z + offset
@@ -153,17 +155,18 @@
 
         @pl.when((other >= 0) & (other <= 3))
         def _():
-            if not finish:
-                arrive(block)
-                send(block, me + sibling, base + step)
-                if not far:
-                    send(block, me + second, 56 + step)
-            else:
-                for copy in copies(block, me + sibling, base + step):
-                    copy.wait_send()
-                if not far:
-                    for copy in copies(block, me + second, 56 + step):
+            for k in range(2):
+                if not finish:
+                    arrive(block, (k,))
+                    if not far:
+                        send(block, me + second, 56 + step, only=(k,))
+                    send(block, me + sibling, base + step, only=(k,))
+                else:
+                    for copy in copies(block, me + sibling, base + step, only=(k,)):
                         copy.wait_send()
+                    if not far:
+                        for copy in copies(block, me + second, 56 + step, only=(k,)):
+                            copy.wait_send()
 
     for finish in (False, True):
         for step in range(len(OFFSETS) + 2):
@@ -231,13 +234,13 @@
     def slot16(block):
         return block // 2
 
-    def targets():
-        for a, b in ((1, 1), (0, 1), (1, 0), (0, 0)):
-            for to in range(4):
-                yield to, a, b
+    half = z // 2
+    goals = (3 - 3 * half, 2 - half, z + 1 - 2 * (z % 2), z)
+    kinds = ((1, 1), (0, 1), (1, 0), (0, 0))
+    orders = [(to, a, b) for to in goals for a, b in kinds]
 
     loads = []
-    for order, (to, a, b) in enumerate(targets()):
+    for order, (to, a, b) in enumerate(orders):
         block = 8 * to + ring + a * first + b * second
         for k in range(2):
             copy = pltpu.make_async_copy(
@@ -263,7 +266,7 @@
             whole[k].at[block], pair[k].at[slot16(block)], k, order, slot16(block), me + sibling
         )
 
-    for order, (to, a, b) in enumerate(targets()):
+    for order, (to, a, b) in enumerate(orders):
         for k in range(2):
             pair_copy(order, to, a, b, k).start()
 
@@ -303,93 +306,114 @@
     def first_copy(to, k, source):
         return remote(source, one[k].at[to], k, 24 + to, 24 + to, me + first)
 
-    orders = list(targets())
-    for order, (to, a, b) in enumerate(orders[:8]):
+    def along(goal, k, upward):
+        slot = goal + (0 if upward else 4)
+        mine = own[k].at[slot16(8 * goal + ring)]
+        return remote(
+            mine, lane[k].at[slot], k, 28 + slot, 28 + slot, me + 8 if upward else me - 8
+        )
+
+    def to_second(step):
+        for kind in (0, 1):
+            to, a, b = orders[4 * step + kind]
+            for k in range(2):
+                mine, theirs = base(4 * step + kind, to, a, b, k)
+                add(k, mine, (mine, theirs))
+                second_copy(to, a, k, mine).start()
+
+    def to_first(step):
+        to, a, b = orders[4 * step + 2]
         for k in range(2):
-            mine, theirs = base(order, to, a, b, k)
-            add(k, mine, (mine, theirs))
-            second_copy(to, a, k, mine).start()
-    for order in range(8, 12):
-        to, a, b = orders[order]
-        for k in range(2):
-            mine, theirs = base(order, to, a, b, k)
+            mine, theirs = base(4 * step + 2, to, a, b, k)
             second_copy(to, a, k, mine).wait_recv()
             add(k, mine, (mine, theirs, two[k].at[2 * to + a]))
             first_copy(to, k, mine).start()
-    for order in range(12, 16):
-        to, a, b = orders[order]
+
+    def to_line(step):
+        to, a, b = orders[4 * step + 3]
         for k in range(2):
-            mine, theirs = base(order, to, a, b, k)
+            mine, theirs = base(4 * step + 3, to, a, b, k)
             second_copy(to, a, k, mine).wait_recv()
             first_copy(to, k, mine).wait_recv()
-            add(k, mine, (mine, theirs, two[k].at[2 * to + a], one[k].at[to]))
-
-    def along(goal, k, upward):
-        slot = 28 + goal + (0 if upward else 4)
-        place_in = goal + (0 if upward else 4)
-        mine = own[k].at[slot16(8 * goal + ring)]
-        return mine, remote(
-            mine, lane[k].at[place_in], k, slot, slot, me + 8 if upward else me - 8
-        )
-
-    for goal in (3, 2, 1):
-        for k in range(2):
-            mine, copy = along(goal, k, True)
-
-            @pl.when(z < goal)
+            sources = (mine, theirs, two[k].at[2 * to + a], one[k].at[to])
+            up, down = along(to, k, True), along(to, k, False)
+            from_below, from_above = lane[k].at[to], lane[k].at[4 + to]
+            if step == 3:
+
+                @pl.when(z == 0)
+                def _():
+                    down.wait_recv()
+                    add(k, final[k], sources + (from_above,))
+
+                @pl.when(z == 3)
+                def _():
+                    up.wait_recv()
+                    add(k, final[k], sources + (from_below,))
+
+                @pl.when((z > 0) & (z < 3))
+                def _():
+                    up.wait_recv()
+                    down.wait_recv()
+                    add(k, final[k], sources + (from_below, from_above))
+
+                continue
+
+            @pl.when(to > z)
             def _():
                 @pl.when(z > 0)
                 def _():
-                    copy.wait_recv()
-                    add(k, mine, (mine, lane[k].at[goal]))
-
-                copy.start()
-
-            down = 3 - goal
-            mine_down, copy_down = along(down, k, False)
-
-            @pl.when(z > down)
+                    up.wait_recv()
+                    add(k, mine, sources + (from_below,))
+
+                @pl.when(z == 0)
+                def _():
+                    add(k, mine, sources)
+
+                up.start()
+
+            @pl.when(to < z)
             def _():
                 @pl.when(z < 3)
                 def _():
-                    copy_down.wait_recv()
-                    add(k, mine_down, (mine_down, lane[k].at[4 + down]))
-
-                copy_down.start()
-
-    for goal in range(4):
-
-        @pl.when(z == goal)
-        def _():
-            for k in range(2):
-                mine = own[k].at[slot16(8 * goal + ring)]
-                sources = [mine]
-                if goal > 0:
-                    along(goal, k, True)[1].wait_recv()
-                    sources.append(lane[k].at[goal])
-                if goal < 3:
-                    along(goal, k, False)[1].wait_recv()
-                    sources.append(lane[k].at[4 + goal])
-                add(k, final[k], sources)
+                    down.wait_recv()
+                    add(k, mine, sources + (from_above,))
+
+                @pl.when(z == 3)
+                def _():
+                    add(k, mine, sources)
+
+                down.start()
+
+    to_second(0)
+    to_second(1)
+    to_second(2)
+    to_first(0)
+    to_second(3)
+    to_first(1)
+    to_line(0)
+    to_first(2)
+    to_line(1)
+    to_first(3)
+    to_line(2)
+    to_line(3)
 
     for order, (to, a, b) in enumerate(orders):
         for k in range(2):
             pair_copy(order, to, a, b, k).wait_send()
             mine = own[k].at[0]
-            if order < 8:
+            if b == 1:
                 second_copy(to, a, k, mine).wait_send()
+            elif a == 1:
+                first_copy(to, k, mine).wait_send()
             elif order < 12:
-                first_copy(to, k, mine).wait_send()
-    for goal in range(4):
-        for k in range(2):
-
-            @pl.when(z < goal)
-            def _():
-                along(goal, k, True)[1].wait_send()
-
-            @pl.when(z > goal)
-            def _():
-                along(goal, k, False)[1].wait_send()
+
+                @pl.when(to > z)
+                def _():
+                    along(to, k, True).wait_send()
+
+                @pl.when(to < z)
+                def _():
+                    along(to, k, False).wait_send()
 
 
 def scatter_blocks(a, b, devices):

time: 282 us -> 238 us (0.84)
  Pallas kernels: 182 us -> 139 us
    pallas_call x1, Pallas kernels: 101 us -> 65.8 us  [scatter_blocks(): pl.pallas_call(scatter_kernel, out_shape=(jax.ShapeDtypeStruct(a.shape[1:...]
    pallas_call x1, Pallas kernels: 80.3 us -> 73.5 us  [gather_blocks(): pl.pallas_call(gather_kernel, out_shape=(jax.ShapeDtypeStruct((devices,)...]
where the time goes in v2:
time: 238 us; the launch traced here: 237 us
  Pallas kernels  139 us (58%)
  matrix products  42.6 us (18%)
  local copies, waits for them, and re-layouts  39.3 us (17%)
  other arithmetic  14.2 us (6%)
    pallas_call x1, Pallas kernels, gather_blocks(): pl.pallas_call(gather_kernel, out_shape=(jax.ShapeDtypeStruct((devices,)...  73.5 us
    pallas_call x1, Pallas kernels, scatter_blocks(): pl.pallas_call(scatter_kernel, out_shape=(jax.ShapeDtypeStruct(a.shape[1:...  65.8 us
    another operation x16, local copies, waits for them, and re-layouts, on_device(): jnp.stack(vectors, 1)  14.8 us
    dot_general x4, matrix products, outer_sum(): return jnp.einsum('td,te->de', left, grad, preferred_element_type=FL)  12.5 us
    dot_general x4, matrix products, project(): return jnp.dot(left, right, preferred_element_type=FL)  11.8 us
    dot_general x4, matrix products, back_project(): return jnp.einsum('te,de->td', grad, right, preferred_element_type=FL)  10.9 us
    unnamed x85, local copies, waits for them, and re-layouts  8.35 us
    concatenate x1, other arithmetic, on_device(): jnp.concatenate([grad_w_in.astype(BF), grad_w_out.astype(BF), grad_w_fc1....  6.85 us

profile of v2, /device:TPU:0, one launch (start us, length us, event | category | flops | bytes accessed | tf_op | source)
XLA Modules:
  0.0 237.3 jit_solution(4854089007490872761)
XLA Ops:
  0.7 0.8 constant_dynamic-update-slice_fusion.5
  1.4 0.8 constant_dynamic-update-slice_fusion.4
  2.2 0.8 constant_dynamic-update-slice_fusion.3
  3.0 0.8 constant_dynamic-update-slice_fusion.2
  3.7 0.9 constant_dynamic-update-slice_fusion.1
  4.7 0.7 copy.128
  5.4 0.7 copy.129
  6.2 0.7 copy.130
  8.4 0.7 copy.133
  10.6 0.7 reshape.139
  11.5 0.9 copy-done
  12.4 73.5 %shard_map.305 = (bf16[32,24,6272]{2,1,0:T(8,128)(2,1)}, bf16[32,96,768]{2,1,0:T(8,128)(2,1)}) custom-call(bf16[24,6272]{1,0:T(8,128)(2,1)S(1)} %constant_dynamic-update-slice_fusion.a_ref, bf16[96,768]{1,0:T(8,128)(2,1)S(1)} %copy-done), custom_call_target="tpu_custom_call" | custom-call | tf_op jit(solution)/shard_map/pallas_call | solution.py:189
  85.9 0.9 slice.112
  87.7 1.1 convert_reduce_fusion
  88.8 1.2 fusion.48
  90.6 3.3 %fusion.10 = bf16[256,2304]{1,0:T(8,128)(2,1)S(1)} fusion(bf16[768,6272]{1,0:T(8,128)(2,1)} %bitcast.79, f32[2304]{0:T(1024)S(1)} %pad_maximum_fusion, bf16[256,768]{1,0:T(8,128)(2,1)} %param.18, f32[768]{0:T(1024)S(1)} %get-tuple-element.47, f32[768]{0:T(1024)S(1)} %get-tuple-element.48, f32[256]{0:T(256)S(1)} %add_rsqrt_fusion.1, ...), kind=kOutput, calls=%fused_computation.15 | convolution fusion | flops 908328960 | bytes 5129216 | tf_op jit(solution)/shard_map/dot_general | solution.py:36
  94.9 1.8 fusion.89
  97.3 1.8 fusion.31
  99.6 1.9 fusion.94
  102.9 4.0 %fusion.7 = f32[256,3072]{1,0:T(8,128)S(1)} fusion(bf16[768,6272]{1,0:T(8,128)(2,1)} %bitcast.81, f32[3072]{0:T(1024)S(1)} %add.116, f32[256,768]{1,0:T(8,128)S(1)} %get-tuple-element.63, f32[768]{0:T(1024)S(1)} %get-tuple-element.43, f32[768]{0:T(1024)S(1)} %get-tuple-element.41, f32[256]{0:T(256)S(1)} %add_rsqrt_fusion, f32[256]{0:T(256)S(1)} %broadcast_multiply_fusion.4), kind=kOutput, calls=%fused_computation.14 | convolution fusion | flops 1209729024 | bytes 8671232 | tf_op jit(solution)/shard_map/dot_general | solution.py:36
  106.9 2.7 %fusion.28 = bf16[256,768]{1,0:T(8,128)(2,1)} fusion(f32[256,768]{1,0:T(8,128)S(1)} %get-tuple-element.63, bf16[3072,768]{1,0:T(8,128)(2,1)S(1)} %bitcast.97, f32[768]{0:T(1024)S(1)} %copy-done.27, f32[256]{0:T(256)S(1)} %compare_convert_fusion, f32[256,3072]{1,0:T(8,128)S(1)} %fusion.7), kind=kOutput, calls=%fused_computation.45 | convolution fusion | flops 1215823872 | bytes 9048064 | tf_op jit(solution)/shard_map/dot_general | solution.py:36
  109.6 4.9 %fusion.95 = (bf16[3072]{0:T(1024)(128)(2,1)}, bf16[256,3072]{1,0:T(8,128)(2,1)S(1)}) fusion(f32[256,3072]{1,0:T(8,128)S(1)} %fusion.7, bf16[3072,768]{1,0:T(8,128)(2,1)S(1)} %bitcast.98, bf16[256,768]{1,0:T(8,128)(2,1)S(1)} %copy-done.6, f32[256]{0:T(256)S(1)} %compare_convert_fusion), kind=kOutput, calls=%fused_computation.148 | convolution fusion | flops 1225061376 | bytes 9837568 | tf_op jit(solution)/shard_map/te,de->td/dot_general | solution.py:40
  114.6 2.1 multiply_reduce_fusion.1
  116.7 1.0 convert_reduce_fusion.1
  118.5 2.1 multiply_reduce_fusion
  124.2 3.4 %fusion.47 = (bf16[768]{0:T(1024)(128)(2,1)S(1)}, f32[256]{0:T(256)S(1)}, f32[256]{0:T(256)S(1)}, bf16[768]{0:T(1024)(128)(2,1)S(1)}, f32[256,768]{1,0:T(8,128)S(1)}) fusion(bf16[256,768]{1,0:T(8,128)(2,1)S(1)} %copy-done.1, f32[256]{0:T(256)S(1)} %copy-done.22, f32[256]{0:T(256)S(1)} %copy-done.16, f32[768]{0:T(1024)S(1)} %get-tuple-element.48, ...), kind=kOutput, calls=%fused_computation.66 | convolution fusion | flops 907933696 | bytes 5908480 | tf_op jit(solution)/shard_map/te,de->td/dot_general | solution.py:40
  127.6 1.2 fusion.46
  128.8 0.8 stack.72
  129.6 0.8 stack.73
  130.5 1.0 reduce
  132.1 0.9 stack.74
  133.0 0.8 stack.75
  133.8 1.5 stack.76
  135.4 1.5 stack.77
  136.9 1.5 stack.78
  138.4 1.2 fusion.49
  139.5 0.9 stack.79
  140.4 1.8 reshape.149
  142.2 2.5 %concatenate.23 = bf16[768,12]{1,0:T(8,128)(2,1)} concatenate(bf16[768,1]{1,0:T(8,128)(2,1)} %stack.72, bf16[768,1]{1,0:T(8,128)(2,1)} %stack.73, bf16[768,1]{1,0:T(8,128)(2,1)} %stack.74, bf16[768,1]{1,0:T(8,128)(2,1)} %stack.75, bf16[768,1]{1,0:T(8,128)(2,1)} %stack.76, bf16[768,1]{1,0:T(8,128)(2,1)} %stack.77, bf16[768,1]{1,0:T(8,128)(2,1)} %stack.78, bf16[768,1]{1,0:T(8,128)(2,1)} %stack.79, ...), dimensions={1} | concatenate | bytes 36864 | tf_op jit(solution)/shard_map/concatenate | solution.py:577
  144.8 5.1 %convolution_convert_fusion.1 = bf16[768,3072]{1,0:T(8,128)(2,1)} fusion(bf16[256,3072]{1,0:T(8,128)(2,1)} %copy-done.8, f32[256,768]{1,0:T(8,128)S(1)} %get-tuple-element.63, f32[768]{0:T(1024)S(1)} %get-tuple-element.43, f32[768]{0:T(1024)S(1)} %get-tuple-element.41, f32[256]{0:T(256)} %copy-done.24, f32[256]{0:T(256)} %copy-done.18), kind=kOutput, calls=%fused_computation.5 | convolution fusion | flops 1211301888 | bytes 7086080 | tf_op jit(solution)/shard_map/td,te->de/dot_general | solution.py:44
  149.9 1.5 convolution_convert_fusion.3
  151.4 2.4 %copy.166 = bf16[768,768]{1,0:T(8,128)(2,1)} copy(bf16[768,768]{0,1:T(8,128)(2,1)} %convolution_convert_fusion.3) | data formatting | bytes 2359296 | tf_op jit(solution)/shard_map/convert_element_type | solution.py:582
  153.9 1.3 convolution_convert_fusion.2
  155.2 0.8 slice-done.1
  156.4 6.8 %fusion.2 = bf16[768,6272]{1,0:T(8,128)(2,1)} fusion(bf16[768,12]{1,0:T(8,128)(2,1)S(1)} %copy-done.9, bf16[768,3072]{1,0:T(8,128)(2,1)S(1)} %bitcast.71, bf16[768,768]{1,0:T(8,128)(2,1)S(1)} %copy-done.2, bf16[768,2304]{1,0:T(8,128)(2,1)S(1)} %convolution_convert_fusion.2), kind=kLoop, calls=%fused_computation.3 | loop fusion | flops 48168960 | bytes 19089408 | tf_op jit(solution)/shard_map/concatenate | solution.py:581
  163.3 4.5 %convolution_convert_fusion = bf16[3072,768]{1,0:T(8,128)(2,1)} fusion(bf16[256,768]{1,0:T(8,128)(2,1)S(1)} %copy-done.7, f32[256]{0:T(256)S(1)} %copy-done.26, f32[256,3072]{1,0:T(8,128)S(1)} %copy-done.30), kind=kOutput, calls=%fused_computation.4 | convolution fusion | flops 1217986560 | bytes 8258560 | tf_op jit(solution)/shard_map/td,te->de/dot_general | solution.py:44
  167.8 65.8 %shard_map.306 = (f32[24,6272]{1,0:T(8,128)S(1)}, f32[96,768]{1,0:T(8,128)S(1)}) custom-call(bf16[32,24,6272]{2,1,0:T(8,128)(2,1)} %bitcast.69, bf16[32,96,768]{2,1,0:T(8,128)(2,1)} %bitcast.72), custom_call_target="tpu_custom_call" | custom-call | tf_op jit(solution)/shard_map/pallas_call | solution.py:430
  233.6 0.8 slice_reduce_fusion
  (129 shorter events, 15.2 us)
Async XLA Ops:
  11.5 0.9 copy-start
  87.0 3.1 %copy-start.13 = (bf16[768,12]{0,1:T(8,128)(2,1)}, bf16[768,12]{0,1:T(8,128)(2,1)S(1)}, u32[]{:S(2)}) copy-start(bf16[768,12]{0,1:T(8,128)(2,1)S(1)} %copy.171) | copy-start | bytes 55300
  88.8 1.3 copy-start.15
  90.1 0.5 copy-start.21
  94.3 2.4 %copy-start.10 = (bf16[2,128,12,64]{1,0,3,2:T(2,128)(2,1)}, bf16[2,128,12,64]{1,0,3,2:T(2,128)(2,1)S(1)}, u32[]{:S(2)}) copy-start(bf16[2,128,12,64]{1,0,3,2:T(2,128)(2,1)S(1)} %reshape.141) | copy-start | bytes 1179652
  94.9 4.2 %copy-start.3 = (bf16[2,128,12,64]{1,0,3,2:T(2,128)(2,1)}, bf16[2,128,12,64]{1,0,3,2:T(2,128)(2,1)S(1)}, u32[]{:S(2)}) copy-start(bf16[2,128,12,64]{1,0,3,2:T(2,128)(2,1)S(1)} %reshape.142) | copy-start | bytes 1179652
  96.7 0.6 copy-start.19
  97.3 2.3 copy-start.1
  97.3 2.3 copy-start.28
  99.2 3.0 %copy-start.14 = (bf16[768,12]{0,1:T(8,128)(2,1)S(1)}, bf16[768,12]{0,1:T(8,128)(2,1)}, u32[]{:S(2)}) copy-start(bf16[768,12]{0,1:T(8,128)(2,1)} %copy-done.13) | copy-start | bytes 55300
  102.1 14.6 %copy-start.25 = (f32[256]{0:T(256)}, f32[256]{0:T(256)S(1)}, u32[]{:S(2)}) copy-start(f32[256]{0:T(256)S(1)} %compare_convert_fusion) | copy-start | bytes 3076
  102.6 14.1 %copy-start.18 = (f32[256]{0:T(256)}, f32[256]{0:T(256)S(1)}, u32[]{:S(2)}) copy-start(f32[256]{0:T(256)S(1)} %broadcast_multiply_fusion.4) | copy-start | bytes 3076
  102.6 4.2 %slice-start.5 = ((s8[4718592]{0:T(1024)(128)(4,1)}), s8[4194304]{0:T(1024)(128)(4,1)S(1)}, s32[]{:S(2)}) async-start(s8[4718592]{0:T(1024)(128)(4,1)} %bitcast.95), calls=%async_computation.5 | async-start | bytes 8388608
  102.8 13.9 %copy-start.24 = (f32[256]{0:T(256)}, f32[256]{0:T(256)S(1)}, u32[]{:S(2)}) copy-start(f32[256]{0:T(256)S(1)} %add_rsqrt_fusion) | copy-start | bytes 3076
  102.8 4.0 %copy-start.27 = (f32[768]{0:T(1024)S(1)}, f32[768]{0:T(1024)}, u32[]{:S(2)}) copy-start(f32[768]{0:T(1024)} %get-tuple-element.42) | copy-start | bytes 9220
  102.9 4.0 %slice-start.6 = ((s8[4718592]{0:T(1024)(128)(4,1)}), s8[524288]{0:T(1024)(128)(4,1)S(1)}, s32[]{:S(2)}) async-start(s8[4718592]{0:T(1024)(128)(4,1)} %bitcast.95), calls=%async_computation.6 | async-start | bytes 1048576
  106.9 2.8 %copy-start.29 = (f32[256,3072]{1,0:T(8,128)}, f32[256,3072]{1,0:T(8,128)S(1)}, u32[]{:S(2)}) copy-start(f32[256,3072]{1,0:T(8,128)S(1)} %fusion.7) | copy-start | bytes 9437188
  106.9 2.8 %copy-start.6 = (bf16[256,768]{1,0:T(8,128)(2,1)S(1)}, bf16[256,768]{1,0:T(8,128)(2,1)}, u32[]{:S(2)}) copy-start(bf16[256,768]{1,0:T(8,128)(2,1)} %param.19) | copy-start | bytes 1179652
  106.9 7.7 %slice-start.2 = ((s8[9633792]{0:T(1024)(128)(4,1)}), s8[4194304]{0:T(1024)(128)(4,1)S(1)}, s32[]{:S(2)}) async-start(s8[9633792]{0:T(1024)(128)(4,1)} %bitcast.83), calls=%async_computation.2 | async-start | bytes 8388608
  106.9 7.6 %slice-start.3 = ((s8[9633792]{0:T(1024)(128)(4,1)}), s8[4194304]{0:T(1024)(128)(4,1)S(1)}, s32[]{:S(2)}) async-start(s8[9633792]{0:T(1024)(128)(4,1)} %bitcast.83), calls=%async_computation.3 | async-start | bytes 8388608
  109.6 4.9 %slice-start.4 = ((s8[9633792]{0:T(1024)(128)(4,1)}), s8[1245184]{0:T(1024)(128)(4,1)S(1)}, s32[]{:S(2)}) async-start(s8[9633792]{0:T(1024)(128)(4,1)} %bitcast.83), calls=%async_computation.4 | async-start | bytes 2490368
  114.5 3.1 %copy-start.8 = (bf16[256,3072]{1,0:T(8,128)(2,1)}, bf16[256,3072]{1,0:T(8,128)(2,1)S(1)}, u32[]{:S(2)}) copy-start(bf16[256,3072]{1,0:T(8,128)(2,1)S(1)} %get-tuple-element.69) | copy-start | bytes 4718596
  118.5 2.1 copy-start.11
  118.5 2.2 copy-start.5
  118.5 2.1 copy-start.20
  120.7 1.2 copy-start.4
  121.0 2.0 copy-start.12
  123.0 1.2 copy-start.16
  123.0 1.2 copy-start.22
  149.9 4.0 %copy-start.17 = (f32[256]{0:T(256)S(1)}, f32[256]{0:T(256)}, u32[]{:S(2)}) copy-start(f32[256]{0:T(256)} %copy-done.15) | copy-start | bytes 3076
  149.9 4.0 %copy-start.23 = (f32[256]{0:T(256)S(1)}, f32[256]{0:T(256)}, u32[]{:S(2)}) copy-start(f32[256]{0:T(256)} %copy-done.21) | copy-start | bytes 3076
  151.4 3.8 %slice-start = ((s8[4718592]{0:T(1024)(128)(4,1)}), s8[524288]{0:T(1024)(128)(4,1)S(1)}, s32[]{:S(2)}) async-start(s8[4718592]{0:T(1024)(128)(4,1)} %bitcast.70), calls=%async_computation | async-start | bytes 1048576
  153.9 2.2 slice-start.1
  153.9 2.5 %copy-start.2 = (bf16[768,768]{1,0:T(8,128)(2,1)S(1)}, bf16[768,768]{1,0:T(8,128)(2,1)}, u32[]{:S(2)}) copy-start(bf16[768,768]{1,0:T(8,128)(2,1)} %copy.166) | copy-start | bytes 3538948
  153.9 2.5 %copy-start.9 = (bf16[768,12]{1,0:T(8,128)(2,1)S(1)}, bf16[768,12]{1,0:T(8,128)(2,1)}, u32[]{:S(2)}) copy-start(bf16[768,12]{1,0:T(8,128)(2,1)} %concatenate.23) | copy-start | bytes 55300
  156.4 6.9 %copy-start.7 = (bf16[256,768]{1,0:T(8,128)(2,1)S(1)}, bf16[256,768]{1,0:T(8,128)(2,1)}, u32[]{:S(2)}) copy-start(bf16[256,768]{1,0:T(8,128)(2,1)} %param.19) | copy-start | bytes 1179652
  156.4 6.9 %copy-start.26 = (f32[256]{0:T(256)S(1)}, f32[256]{0:T(256)}, u32[]{:S(2)}) copy-start(f32[256]{0:T(256)} %copy-done.25) | copy-start | bytes 3076
  156.4 6.9 %copy-start.30 = (f32[256,3072]{1,0:T(8,128)S(1)}, f32[256,3072]{1,0:T(8,128)}, u32[]{:S(2)}) copy-start(f32[256,3072]{1,0:T(8,128)} %copy-done.29) | copy-start | bytes 9437188

commit v3 on v2

--- a/solution.py
+++ b/solution.py
@@ -482,20 +482,31 @@
     vectors = (ln1_gain, ln1_bias, b_query, b_value, b_out, ln2_gain, ln2_bias, b_fc2)
     few = len(vectors)
     per_row = b_fc1.shape[0] // depth
-    small = jnp.concatenate(
-        [jnp.stack(vectors, 1), b_fc1.reshape(depth, per_row)], axis=1
-    )
-    small = jnp.pad(small, ((0, 0), (0, LANES - small.shape[1])))
+    as_rows = depth > few and per_row * depth <= LANES
+    if as_rows:
+        lines = [jnp.pad(v[None, :], ((0, 0), (0, LANES - depth))) for v in vectors]
+        lines.append(jnp.pad(b_fc1[None, :], ((0, 0), (0, LANES - per_row * depth))))
+        small = jnp.concatenate(lines, axis=0)
+        small = jnp.pad(small, ((0, depth - few - 1), (0, 0)))
+    else:
+        small = jnp.concatenate([jnp.stack(vectors, 1), b_fc1.reshape(depth, per_row)], axis=1)
+        small = jnp.pad(small, ((0, 0), (0, LANES - small.shape[1])))
     block_a = jnp.concatenate([w_query, w_key, w_value, w_out, w_fc1, small], axis=1)
     all_a, all_b = gather_blocks(block_a, w_fc2, devices)
+    small = all_a[:, :, wide:]
     all_a = all_a.reshape(width, wide + LANES)
     w_in = all_a[:, : 3 * width]
     w_out = all_a[:, 3 * width : 4 * width]
     w_fc1 = all_a[:, 4 * width : wide]
     w_fc2 = all_b.reshape(hidden, width)
-    small = all_a[:, wide : wide + few + per_row].astype(FL)
-    ln1_gain, ln1_bias, b_query, b_value, b_out, ln2_gain, ln2_bias, b_fc2 = small[:, :few].T
-    b_fc1 = small[:, few:].reshape(hidden)
+    if as_rows:
+        table = small[:, :few, :depth].astype(FL).transpose(1, 0, 2).reshape(few, width)
+        b_fc1 = small[:, few, : per_row * depth].astype(FL).reshape(hidden)
+    else:
+        small = small.reshape(width, LANES).astype(FL)
+        table = small[:, :few].T
+        b_fc1 = small[:, few : few + per_row].reshape(hidden)
+    ln1_gain, ln1_bias, b_query, b_value, b_out, ln2_gain, ln2_bias, b_fc2 = table
 
     live = (jnp.arange(rows, dtype=jnp.int32) // LENGTH < counts[0]).astype(FL)[:, None]
     inputs = tokens.astype(FL)
@@ -574,10 +585,16 @@
         grad_ln2_bias,
         column_sums(grad_out),
     )
-    small = jnp.concatenate(
-        [jnp.stack(vectors, 1), column_sums(grad_pre.astype(FL)).reshape(width, per_row)], axis=1
-    )
-    small = jnp.pad(small, ((0, 0), (0, LANES - small.shape[1])))
+    pre_sums = column_sums(grad_pre.astype(FL))
+    if as_rows:
+        table = jnp.stack(vectors, 0).astype(BF).reshape(few, devices, depth).transpose(1, 0, 2)
+        table = jnp.pad(table, ((0, 0), (0, depth - few), (0, LANES - depth)))
+        line = pre_sums.astype(BF).reshape(devices, 1, per_row * depth)
+        line = jnp.pad(line, ((0, 0), (few, depth - few - 1), (0, LANES - per_row * depth)))
+        small = (table + line).reshape(width, LANES)
+    else:
+        small = jnp.concatenate([jnp.stack(vectors, 1), pre_sums.reshape(width, per_row)], axis=1)
+        small = jnp.pad(small, ((0, 0), (0, LANES - small.shape[1])))
     sums_a = jnp.concatenate(
         [grad_w_in.astype(BF), grad_w_out.astype(BF), grad_w_fc1.astype(BF), small.astype(BF)],
         axis=1,
@@ -587,8 +604,13 @@
         grad_w_fc2.astype(BF).reshape((devices,) + (hidden // devices, width)),
         devices,
     )
-    small = got_a[:, wide : wide + few + per_row]
-    columns = tuple(small[:, i] for i in range(few))
+    if as_rows:
+        columns = tuple(got_a[i, wide : wide + depth] for i in range(few))
+        grad_b_fc1 = got_a[few, wide : wide + per_row * depth]
+    else:
+        small = got_a[:, wide : wide + few + per_row]
+        columns = tuple(small[:, i] for i in range(few))
+        grad_b_fc1 = small[:, few:].reshape(hidden // devices)
     return (
         mixed,
         grad_tokens,
@@ -604,7 +626,7 @@
         columns[5],
         columns[6],
         got_a[:, 4 * width : wide],
-        small[:, few:].reshape(hidden // devices),
+        grad_b_fc1,
         got_b,
         columns[7],
     )

time: 238 us -> 231 us (0.971)
  local copies, waits for them, and re-layouts: 39.3 us -> 33.6 us
  matrix products: 42.6 us -> 40 us
    pad x0 -> x9, local copies, waits for them, and re-layouts: none -> 5.95 us  [the longest x8 5.29 us: on_device(): lines = [jnp.pad(v[None, :], ((0, 0), (0, LANES - depth))) for v in vectors]]
    dot_general x4, matrix products: 12.5 us -> 9.31 us  [outer_sum(): return jnp.einsum('td,te->de', left, grad, preferred_element_type=FL)]
    concatenate x2 -> x1, local copies, waits for them, and re-layouts: 2.64 us -> 0.05 us  [on_device(): small = jnp.concatenate(lines, axis=0)]
    concatenate x1, other arithmetic: 6.85 us -> 4.29 us  [on_device(): jnp.concatenate([grad_w_in.astype(BF), grad_w_out.astype(BF), grad_w_fc1....]
    unnamed x85 -> x68, local copies, waits for them, and re-layouts: 8.35 us -> 5.9 us
    another operation x16 -> x9, local copies, waits for them, and re-layouts: 14.8 us -> 12.6 us  [on_device(): jnp.stack(vectors, 0).astype(BF).reshape(few, devices, depth)]
where the time goes in v3:
time: 231 us; the launch traced here: 230 us
  Pallas kernels  139 us (60%)
  matrix products  40 us (17%)
  local copies, waits for them, and re-layouts  33.6 us (15%)
  other arithmetic  14.8 us (6%)
    pallas_call x1, Pallas kernels, gather_blocks(): pl.pallas_call(gather_kernel, out_shape=(jax.ShapeDtypeStruct((devices,)...  73.5 us
    pallas_call x1, Pallas kernels, scatter_blocks(): pl.pallas_call(scatter_kernel, out_shape=(jax.ShapeDtypeStruct(a.shape[1:...  65.8 us
    another operation x9, local copies, waits for them, and re-layouts, on_device(): jnp.stack(vectors, 0).astype(BF).reshape(few, devices, depth)  12.6 us
    dot_general x4, matrix products, project(): return jnp.dot(left, right, preferred_element_type=FL)  11.8 us
    dot_general x4, matrix products, back_project(): return jnp.einsum('te,de->td', grad, right, preferred_element_type=FL)  11.5 us
    dot_general x4, matrix products, outer_sum(): return jnp.einsum('td,te->de', left, grad, preferred_element_type=FL)  9.31 us
    unnamed x68, local copies, waits for them, and re-layouts  5.9 us
    pad x8, local copies, waits for them, and re-layouts, on_device(): lines = [jnp.pad(v[None, :], ((0, 0), (0, LANES - depth))) for v in vectors]  5.29 us

profile of v3, /device:TPU:0, one launch (start us, length us, event | category | flops | bytes accessed | tf_op | source)
XLA Modules:
  0.0 229.6 jit_solution(2733033900176973061)
XLA Ops:
  0.7 0.8 constant_dynamic-update-slice_fusion.5
  1.4 0.8 constant_dynamic-update-slice_fusion.4
  2.2 0.8 constant_dynamic-update-slice_fusion.3
  3.0 0.8 constant_dynamic-update-slice_fusion.2
  3.7 0.9 constant_dynamic-update-slice_fusion.1
  4.7 0.7 pad.41
  5.3 0.7 pad.42
  6.0 0.7 pad.43
  10.7 0.9 copy-done
  11.6 73.5 %shard_map.305 = (bf16[32,24,6272]{2,1,0:T(8,128)(2,1)}, bf16[32,96,768]{2,1,0:T(8,128)(2,1)}) custom-call(bf16[24,6272]{1,0:T(8,128)(2,1)S(1)} %constant_dynamic-update-slice_fusion.a_ref, bf16[96,768]{1,0:T(8,128)(2,1)S(1)} %copy-done), custom_call_target="tpu_custom_call" | custom-call | tf_op jit(solution)/shard_map/pallas_call | solution.py:189
  85.1 0.9 convert_bitcast_fusion
  86.8 1.1 convert_reduce_fusion
  87.9 1.2 fusion.46
  89.2 3.3 %fusion.8 = bf16[256,2304]{1,0:T(8,128)(2,1)S(1)} fusion(bf16[768,6272]{1,0:T(8,128)(2,1)} %bitcast.101, f32[2304]{0:T(1024)S(1)} %pad_maximum_fusion.1, bf16[256,768]{1,0:T(8,128)(2,1)} %param.18, f32[768]{0:T(1024)S(1)} %add.124, f32[768]{0:T(1024)S(1)} %mul.176, f32[256]{0:T(256)S(1)} %add_rsqrt_fusion.1, f32[256]{0:T(256)S(1)} %broadcast_multiply_fusion.5), kind=kOutput, calls=%fused_computation.13 | convolution fusion | flops 908328960 | bytes 5129216 | tf_op jit(solution)/shard_map/dot_general | solution.py:36
  93.5 1.8 fusion.87
  95.3 1.8 fusion.29
  97.6 1.9 fusion.92
  100.2 0.9 convert_reduce_fusion.1
  101.6 4.0 %fusion.5 = f32[256,3072]{1,0:T(8,128)S(1)} fusion(bf16[768,6272]{1,0:T(8,128)(2,1)} %bitcast.103, f32[3072]{0:T(1024)S(1)} %reshape.207, f32[256,768]{1,0:T(8,128)S(1)} %get-tuple-element.63, f32[768]{0:T(1024)S(1)} %add.134, f32[768]{0:T(1024)S(1)} %mul.184, f32[256]{0:T(256)S(1)} %add_rsqrt_fusion, f32[256]{0:T(256)S(1)} %broadcast_multiply_fusion.4), kind=kOutput, calls=%fused_computation.12 | convolution fusion | flops 1209729024 | bytes 8671232 | tf_op jit(solution)/shard_map/dot_general | solution.py:36
  105.6 2.7 %fusion.26 = bf16[256,768]{1,0:T(8,128)(2,1)} fusion(f32[256,768]{1,0:T(8,128)S(1)} %get-tuple-element.63, bf16[3072,768]{1,0:T(8,128)(2,1)S(1)} %bitcast.111, f32[768]{0:T(1024)S(1)} %add.142, f32[256]{0:T(256)S(1)} %compare_convert_fusion, f32[256,3072]{1,0:T(8,128)S(1)} %fusion.5), kind=kOutput, calls=%fused_computation.43 | convolution fusion | flops 1215823872 | bytes 9048064 | tf_op jit(solution)/shard_map/dot_general | solution.py:36
  108.4 4.9 %fusion.93 = (bf16[3072]{0:T(1024)(128)(2,1)}, bf16[256,3072]{1,0:T(8,128)(2,1)S(1)}) fusion(f32[256,3072]{1,0:T(8,128)S(1)} %fusion.5, bf16[3072,768]{1,0:T(8,128)(2,1)S(1)} %bitcast.112, bf16[256,768]{1,0:T(8,128)(2,1)S(1)} %copy-done.5, f32[256]{0:T(256)S(1)} %compare_convert_fusion), kind=kOutput, calls=%fused_computation.149 | convolution fusion | flops 1225061376 | bytes 9837568 | tf_op jit(solution)/shard_map/te,de->td/dot_general | solution.py:40
  113.3 2.1 multiply_reduce_fusion.1
  115.4 0.9 convert_reduce_fusion.2
  117.2 2.1 multiply_reduce_fusion
  122.9 4.0 %fusion.45 = (bf16[768]{0:T(1024)(128)(2,1)}, f32[256]{0:T(256)S(1)}, f32[256]{0:T(256)S(1)}, bf16[768]{0:T(1024)(128)(2,1)}, f32[256,768]{1,0:T(8,128)S(1)}) fusion(bf16[256,768]{1,0:T(8,128)(2,1)S(1)} %copy-done.1, f32[256]{0:T(256)S(1)} %copy-done.18, f32[256]{0:T(256)S(1)} %copy-done.12, f32[768]{0:T(1024)S(1)} %mul.176, ...), kind=kOutput, calls=%fused_computation.64 | convolution fusion | flops 907933696 | bytes 5908480 | tf_op jit(solution)/shard_map/te,de->td/dot_general | solution.py:40
  126.8 1.2 fusion.44
  128.0 1.4 reshape.208
  129.4 1.4 stack.36
  130.8 1.4 stack.37
  132.2 1.0 reduce.1
  133.1 1.3 fusion.86
  134.4 1.4 stack.38
  135.8 1.3 stack.39
  137.1 1.3 stack.40
  138.4 1.4 stack.41
  139.8 1.4 stack.42
  141.2 1.7 fusion.47
  142.9 1.4 stack.43
  144.3 1.7 stack.35
  145.9 0.9 pad_add_fusion
  146.9 3.0 %convolution_convert_fusion.1 = bf16[768,3072]{1,0:T(8,128)(2,1)S(1)} fusion(bf16[256,3072]{1,0:T(8,128)(2,1)} %copy-done.7, f32[256,768]{1,0:T(8,128)S(1)} %get-tuple-element.63, f32[768]{0:T(1024)S(1)} %add.134, f32[768]{0:T(1024)S(1)} %mul.184, f32[256]{0:T(256)} %copy-done.20, f32[256]{0:T(256)} %copy-done.14), kind=kOutput, calls=%fused_computation.3 | convolution fusion | flops 1211301888 | bytes 7086080 | tf_op jit(solution)/shard_map/td,te->de/dot_general | solution.py:44
  150.4 1.3 convolution_convert_fusion.2
  151.7 4.3 %pad_maximum_fusion.a_ref = bf16[32,24,6272]{2,1,0:T(8,128)(2,1)} fusion(bf16[32,24,128]{2,1,0:T(8,128)(2,1)S(1)} %pad_add_fusion, bf16[32,24,3072]{2,1,0:T(8,128)(2,1)S(1)} %bitcast.91, bf16[32,24,768]{2,1,0:T(8,128)(2,1)S(1)} %bitcast.93, bf16[32,24,2304]{2,1,0:T(8,128)(2,1)S(1)} %bitcast.92), kind=kLoop, calls=%fused_computation.1 | loop fusion | flops 38535168 | bytes 19267584 | tf_op jit(solution)/shard_map/concatenate | solution.py:598
  156.0 4.5 %convolution_convert_fusion = bf16[3072,768]{1,0:T(8,128)(2,1)} fusion(bf16[256,768]{1,0:T(8,128)(2,1)S(1)} %copy-done.6, f32[256]{0:T(256)S(1)} %copy-done.22, f32[256,3072]{1,0:T(8,128)S(1)} %copy-done.24), kind=kOutput, calls=%fused_computation.2 | convolution fusion | flops 1217986560 | bytes 8258560 | tf_op jit(solution)/shard_map/td,te->de/dot_general | solution.py:44
  160.6 65.8 %shard_map.306 = (f32[24,6272]{1,0:T(8,128)S(1)}, f32[96,768]{1,0:T(8,128)S(1)}) custom-call(bf16[32,24,6272]{2,1,0:T(8,128)(2,1)} %pad_maximum_fusion.a_ref, bf16[32,96,768]{2,1,0:T(8,128)(2,1)} %bitcast.94), custom_call_target="tpu_custom_call" | custom-call | tf_op jit(solution)/shard_map/pallas_call | solution.py:430
  226.9 0.7 fusion.85
  227.6 0.7 slice.118
  228.8 0.7 copy.138
  (115 shorter events, 12.6 us)
Async XLA Ops:
  10.7 0.9 copy-start
  87.9 4.6 %copy-start.11 = (f32[256]{0:T(256)}, f32[256]{0:T(256)S(1)}, u32[]{:S(2)}) copy-start(f32[256]{0:T(256)S(1)} %broadcast_multiply_fusion.5) | copy-start | bytes 3076
  89.2 3.3 %copy-start.17 = (f32[256]{0:T(256)}, f32[256]{0:T(256)S(1)}, u32[]{:S(2)}) copy-start(f32[256]{0:T(256)S(1)} %add_rsqrt_fusion.1) | copy-start | bytes 3076
  92.9 2.4 %copy-start.8 = (bf16[2,128,12,64]{1,0,3,2:T(2,128)(2,1)}, bf16[2,128,12,64]{1,0,3,2:T(2,128)(2,1)S(1)}, u32[]{:S(2)}) copy-start(bf16[2,128,12,64]{1,0,3,2:T(2,128)(2,1)S(1)} %reshape.197) | copy-start | bytes 1179652
  93.5 3.6 %copy-start.2 = (bf16[2,128,12,64]{1,0,3,2:T(2,128)(2,1)}, bf16[2,128,12,64]{1,0,3,2:T(2,128)(2,1)S(1)}, u32[]{:S(2)}) copy-start(bf16[2,128,12,64]{1,0,3,2:T(2,128)(2,1)S(1)} %reshape.198) | copy-start | bytes 1179652
  95.3 2.2 copy-start.15
  95.3 2.2 copy-start.1
  100.2 15.3 %copy-start.21 = (f32[256]{0:T(256)}, f32[256]{0:T(256)S(1)}, u32[]{:S(2)}) copy-start(f32[256]{0:T(256)S(1)} %compare_convert_fusion) | copy-start | bytes 3076
  101.3 14.1 %copy-start.14 = (f32[256]{0:T(256)}, f32[256]{0:T(256)S(1)}, u32[]{:S(2)}) copy-start(f32[256]{0:T(256)S(1)} %broadcast_multiply_fusion.4) | copy-start | bytes 3076
  101.3 4.2 %slice-start.3 = ((s8[4718592]{0:T(1024)(128)(4,1)}), s8[4194304]{0:T(1024)(128)(4,1)S(1)}, s32[]{:S(2)}) async-start(s8[4718592]{0:T(1024)(128)(4,1)} %bitcast.109), calls=%async_computation.3 | async-start | bytes 8388608
  101.6 13.9 %copy-start.20 = (f32[256]{0:T(256)}, f32[256]{0:T(256)S(1)}, u32[]{:S(2)}) copy-start(f32[256]{0:T(256)S(1)} %add_rsqrt_fusion) | copy-start | bytes 3076
  101.6 4.0 %slice-start.4 = ((s8[4718592]{0:T(1024)(128)(4,1)}), s8[524288]{0:T(1024)(128)(4,1)S(1)}, s32[]{:S(2)}) async-start(s8[4718592]{0:T(1024)(128)(4,1)} %bitcast.109), calls=%async_computation.4 | async-start | bytes 1048576
  105.6 2.8 %copy-start.23 = (f32[256,3072]{1,0:T(8,128)}, f32[256,3072]{1,0:T(8,128)S(1)}, u32[]{:S(2)}) copy-start(f32[256,3072]{1,0:T(8,128)S(1)} %fusion.5) | copy-start | bytes 9437188
  105.6 2.8 %copy-start.5 = (bf16[256,768]{1,0:T(8,128)(2,1)S(1)}, bf16[256,768]{1,0:T(8,128)(2,1)}, u32[]{:S(2)}) copy-start(bf16[256,768]{1,0:T(8,128)(2,1)} %param.19) | copy-start | bytes 1179652
  105.6 7.6 %slice-start = ((s8[9633792]{0:T(1024)(128)(4,1)}), s8[4194304]{0:T(1024)(128)(4,1)S(1)}, s32[]{:S(2)}) async-start(s8[9633792]{0:T(1024)(128)(4,1)} %bitcast.105), calls=%async_computation | async-start | bytes 8388608
  105.6 7.6 %slice-start.1 = ((s8[9633792]{0:T(1024)(128)(4,1)}), s8[4194304]{0:T(1024)(128)(4,1)S(1)}, s32[]{:S(2)}) async-start(s8[9633792]{0:T(1024)(128)(4,1)} %bitcast.105), calls=%async_computation.1 | async-start | bytes 8388608
  108.4 4.9 %slice-start.2 = ((s8[9633792]{0:T(1024)(128)(4,1)}), s8[1245184]{0:T(1024)(128)(4,1)S(1)}, s32[]{:S(2)}) async-start(s8[9633792]{0:T(1024)(128)(4,1)} %bitcast.105), calls=%async_computation.2 | async-start | bytes 2490368
  113.3 2.2 copy-start.7
  117.2 2.1 copy-start.9
  117.2 2.2 copy-start.4
  117.2 2.1 copy-start.16
  119.3 1.2 copy-start.3
  119.7 2.0 copy-start.10
  121.7 1.2 copy-start.12
  121.7 1.2 copy-start.18
  146.8 3.5 %copy-start.13 = (f32[256]{0:T(256)S(1)}, f32[256]{0:T(256)}, u32[]{:S(2)}) copy-start(f32[256]{0:T(256)} %copy-done.11) | copy-start | bytes 3076
  146.9 3.5 %copy-start.19 = (f32[256]{0:T(256)S(1)}, f32[256]{0:T(256)}, u32[]{:S(2)}) copy-start(f32[256]{0:T(256)} %copy-done.17) | copy-start | bytes 3076
  151.7 4.3 %copy-start.6 = (bf16[256,768]{1,0:T(8,128)(2,1)S(1)}, bf16[256,768]{1,0:T(8,128)(2,1)}, u32[]{:S(2)}) copy-start(bf16[256,768]{1,0:T(8,128)(2,1)} %param.19) | copy-start | bytes 1179652
  151.7 4.3 %copy-start.22 = (f32[256]{0:T(256)S(1)}, f32[256]{0:T(256)}, u32[]{:S(2)}) copy-start(f32[256]{0:T(256)} %copy-done.21) | copy-start | bytes 3076
  151.7 4.3 %copy-start.24 = (f32[256,3072]{1,0:T(8,128)S(1)}, f32[256,3072]{1,0:T(8,128)}, u32[]{:S(2)}) copy-start(f32[256,3072]{1,0:T(8,128)} %copy-done.23) | copy-start | bytes 9437188

commit v4 on v3

--- a/solution.py
+++ b/solution.py
@@ -484,14 +484,19 @@
     per_row = b_fc1.shape[0] // depth
     as_rows = depth > few and per_row * depth <= LANES
     if as_rows:
-        lines = [jnp.pad(v[None, :], ((0, 0), (0, LANES - depth))) for v in vectors]
-        lines.append(jnp.pad(b_fc1[None, :], ((0, 0), (0, LANES - per_row * depth))))
-        small = jnp.concatenate(lines, axis=0)
-        small = jnp.pad(small, ((0, depth - few - 1), (0, 0)))
+        small = sum(
+            jnp.pad(v[None, :], ((i, depth - 1 - i), (0, LANES - v.shape[0])))
+            for i, v in enumerate(vectors + (b_fc1,))
+        )
     else:
         small = jnp.concatenate([jnp.stack(vectors, 1), b_fc1.reshape(depth, per_row)], axis=1)
         small = jnp.pad(small, ((0, 0), (0, LANES - small.shape[1])))
-    block_a = jnp.concatenate([w_query, w_key, w_value, w_out, w_fc1, small], axis=1)
+    pieces = (w_query, w_key, w_value, w_out, w_fc1, small)
+    starts = (0, width, 2 * width, 3 * width, 4 * width, wide)
+    block_a = sum(
+        jnp.pad(piece, ((0, 0), (start, wide + LANES - start - piece.shape[1])))
+        for start, piece in zip(starts, pieces)
+    )
     all_a, all_b = gather_blocks(block_a, w_fc2, devices)
     small = all_a[:, :, wide:]
     all_a = all_a.reshape(width, wide + LANES)
@@ -587,7 +592,8 @@
     )
     pre_sums = column_sums(grad_pre.astype(FL))
     if as_rows:
-        table = jnp.stack(vectors, 0).astype(BF).reshape(few, devices, depth).transpose(1, 0, 2)
+        table = lax.optimization_barrier(jnp.stack(vectors, 0))
+        table = table.reshape(few, devices, depth).transpose(1, 0, 2).astype(BF)
         table = jnp.pad(table, ((0, 0), (0, depth - few), (0, LANES - depth)))
         line = pre_sums.astype(BF).reshape(devices, 1, per_row * depth)
         line = jnp.pad(line, ((0, 0), (few, depth - few - 1), (0, LANES - per_row * depth)))

time: 231 us -> 219 us (0.948)
  local copies, waits for them, and re-layouts: 33.6 us -> 23.2 us
    pad x9 -> x0, local copies, waits for them, and re-layouts: 5.95 us -> none  [the longest x8 5.29 us: on_device(): lines = [jnp.pad(v[None, :], ((0, 0), (0, LANES - depth))) for v in vectors]]
    unnamed x68 -> x63, local copies, waits for them, and re-layouts: 5.9 us -> 3.06 us
    another operation x9, local copies, waits for them, and re-layouts: 12.6 us -> 10 us  [on_device(): table = lax.optimization_barrier(jnp.stack(vectors, 0))]
    convert_element_type x0 -> x2, local copies, waits for them, and re-layouts: none -> 2.33 us  [on_device(): table = table.reshape(few, devices, depth).transpose(1, 0, 2).astype(BF)]
where the time goes in v4:
time: 219 us
  Pallas kernels  139 us (63%)
  matrix products  40 us (18%)
  local copies, waits for them, and re-layouts  23.2 us (11%)
  other arithmetic  14.1 us (6%)
    pallas_call x1, Pallas kernels, gather_blocks(): pl.pallas_call(gather_kernel, out_shape=(jax.ShapeDtypeStruct((devices,)...  73.5 us
    pallas_call x1, Pallas kernels, scatter_blocks(): pl.pallas_call(scatter_kernel, out_shape=(jax.ShapeDtypeStruct(a.shape[1:...  65.8 us
    dot_general x4, matrix products, project(): return jnp.dot(left, right, preferred_element_type=FL)  11.8 us
    dot_general x4, matrix products, back_project(): return jnp.einsum('te,de->td', grad, right, preferred_element_type=FL)  11.5 us
    another operation x9, local copies, waits for them, and re-layouts, on_device(): table = lax.optimization_barrier(jnp.stack(vectors, 0))  10 us
    dot_general x4, matrix products, outer_sum(): return jnp.einsum('td,te->de', left, grad, preferred_element_type=FL)  9.28 us

profile of v4, /device:TPU:0, one launch (start us, length us, event | category | flops | bytes accessed | tf_op | source)
XLA Modules:
  0.0 218.5 jit_solution(9947775671177621752)
XLA Ops:
  0.7 0.8 pad_add_fusion.2
  1.5 0.9 pad_add_fusion.a_ref
  2.4 0.9 copy-done
  3.3 73.5 %shard_map.305 = (bf16[32,24,6272]{2,1,0:T(8,128)(2,1)}, bf16[32,96,768]{2,1,0:T(8,128)(2,1)}) custom-call(bf16[24,6272]{1,0:T(8,128)(2,1)S(1)} %pad_add_fusion.a_ref, bf16[96,768]{1,0:T(8,128)(2,1)S(1)} %copy-done), custom_call_target="tpu_custom_call" | custom-call | tf_op jit(solution)/shard_map/pallas_call | solution.py:189
  76.8 0.9 convert_bitcast_fusion
  78.5 1.1 convert_reduce_fusion.1
  79.6 1.2 fusion.46
  80.9 0.6 copy-done.17
  81.5 3.3 %fusion.8 = bf16[256,2304]{1,0:T(8,128)(2,1)S(1)} fusion(bf16[768,6272]{1,0:T(8,128)(2,1)} %bitcast.103, f32[2304]{0:T(1024)S(1)} %pad_maximum_fusion.1, bf16[256,768]{1,0:T(8,128)(2,1)} %param.18, f32[768]{0:T(1024)S(1)} %add.186, f32[768]{0:T(1024)S(1)} %mul.176, f32[256]{0:T(256)S(1)} %add_rsqrt_fusion.1, f32[256]{0:T(256)S(1)} %broadcast_multiply_fusion.5), kind=kOutput, calls=%fused_computation.13 | convolution fusion | flops 908328960 | bytes 5129216 | tf_op jit(solution)/shard_map/dot_general | solution.py:36
  85.8 1.8 fusion.87
  87.6 0.6 copy-done.15
  88.2 1.8 fusion.29
  90.4 1.9 fusion.92
  93.1 0.9 convert_reduce_fusion.3
  94.5 4.0 %fusion.5 = f32[256,3072]{1,0:T(8,128)S(1)} fusion(bf16[768,6272]{1,0:T(8,128)(2,1)} %bitcast.105, f32[3072]{0:T(1024)S(1)} %reshape.172, f32[256,768]{1,0:T(8,128)S(1)} %get-tuple-element.64, f32[768]{0:T(1024)S(1)} %add.196, f32[768]{0:T(1024)S(1)} %mul.184, f32[256]{0:T(256)S(1)} %add_rsqrt_fusion, f32[256]{0:T(256)S(1)} %broadcast_multiply_fusion.4), kind=kOutput, calls=%fused_computation.12 | convolution fusion | flops 1209729024 | bytes 8671232 | tf_op jit(solution)/shard_map/dot_general | solution.py:36
  98.5 2.7 %fusion.26 = bf16[256,768]{1,0:T(8,128)(2,1)} fusion(f32[256,768]{1,0:T(8,128)S(1)} %get-tuple-element.64, bf16[3072,768]{1,0:T(8,128)(2,1)S(1)} %bitcast.122, f32[768]{0:T(1024)S(1)} %add.204, f32[256]{0:T(256)S(1)} %compare_convert_fusion, f32[256,3072]{1,0:T(8,128)S(1)} %fusion.5), kind=kOutput, calls=%fused_computation.44 | convolution fusion | flops 1215823872 | bytes 9048064 | tf_op jit(solution)/shard_map/dot_general | solution.py:36
  101.2 4.9 %fusion.93 = (bf16[3072]{0:T(1024)(128)(2,1)}, bf16[256,3072]{1,0:T(8,128)(2,1)S(1)}) fusion(f32[256,3072]{1,0:T(8,128)S(1)} %fusion.5, bf16[3072,768]{1,0:T(8,128)(2,1)S(1)} %bitcast.123, bf16[256,768]{1,0:T(8,128)(2,1)S(1)} %copy-done.6, f32[256]{0:T(256)S(1)} %compare_convert_fusion), kind=kOutput, calls=%fused_computation.147 | convolution fusion | flops 1225061376 | bytes 9837568 | tf_op jit(solution)/shard_map/te,de->td/dot_general | solution.py:40
  106.2 2.1 multiply_reduce_fusion.1
  108.3 1.0 convert_reduce_fusion.2
  109.3 0.5 convolution_convert_fusion.5
  110.1 2.1 multiply_reduce_fusion
  113.5 0.6 fusion.27
  114.7 0.7 fusion.30
  115.8 4.0 %fusion.45 = (bf16[768]{0:T(1024)(128)(2,1)}, f32[256]{0:T(256)S(1)}, f32[256]{0:T(256)S(1)}, bf16[768]{0:T(1024)(128)(2,1)}, f32[256,768]{1,0:T(8,128)S(1)}) fusion(bf16[256,768]{1,0:T(8,128)(2,1)S(1)} %copy-done.1, f32[256]{0:T(256)S(1)} %copy-done.18, f32[256]{0:T(256)S(1)} %copy-done.12, f32[768]{0:T(1024)S(1)} %mul.176, ...), kind=kOutput, calls=%fused_computation.65 | convolution fusion | flops 907933696 | bytes 5908480 | tf_op jit(solution)/shard_map/te,de->td/dot_general | solution.py:40
  119.8 1.2 fusion.44
  121.0 1.4 reshape.173
  122.3 1.3 stack.27
  123.6 1.3 stack.28
  125.3 0.6 stack.29
  125.8 0.6 stack.30
  126.4 1.2 stack.31
  127.7 1.2 stack.32
  128.9 1.2 stack.33
  130.1 1.3 stack.34
  131.4 1.4 stack.35
  132.8 1.5 convert_element_type.178
  134.2 0.9 copy.123
  135.1 0.8 pad_add_fusion.1
  135.9 3.0 %convolution_convert_fusion.1 = bf16[768,3072]{1,0:T(8,128)(2,1)S(1)} fusion(bf16[256,3072]{1,0:T(8,128)(2,1)} %copy-done.5, f32[256,768]{1,0:T(8,128)S(1)} %get-tuple-element.64, f32[768]{0:T(1024)S(1)} %add.196, f32[768]{0:T(1024)S(1)} %mul.184, f32[256]{0:T(256)} %copy-done.20, f32[256]{0:T(256)} %copy-done.14), kind=kOutput, calls=%fused_computation.3 | convolution fusion | flops 1211301888 | bytes 7086080 | tf_op jit(solution)/shard_map/td,te->de/dot_general | solution.py:44
  139.4 1.3 convolution_convert_fusion.2
  140.7 4.3 %pad_maximum_fusion.a_ref = bf16[32,24,6272]{2,1,0:T(8,128)(2,1)} fusion(bf16[32,24,128]{2,1,0:T(8,128)(2,1)S(1)} %pad_add_fusion.1, bf16[32,24,3072]{2,1,0:T(8,128)(2,1)S(1)} %bitcast.93, bf16[32,24,768]{2,1,0:T(8,128)(2,1)S(1)} %bitcast.95, bf16[32,24,2304]{2,1,0:T(8,128)(2,1)S(1)} %bitcast.94), kind=kLoop, calls=%fused_computation.1 | loop fusion | flops 38535168 | bytes 19267584 | tf_op jit(solution)/shard_map/concatenate | solution.py:604
  145.0 4.5 %convolution_convert_fusion = bf16[3072,768]{1,0:T(8,128)(2,1)} fusion(bf16[256,768]{1,0:T(8,128)(2,1)S(1)} %copy-done.7, f32[256]{0:T(256)S(1)} %copy-done.22, f32[256,3072]{1,0:T(8,128)S(1)} %copy-done.24), kind=kOutput, calls=%fused_computation.2 | convolution fusion | flops 1217986560 | bytes 8258560 | tf_op jit(solution)/shard_map/td,te->de/dot_general | solution.py:44
  149.6 65.8 %shard_map.306 = (f32[24,6272]{1,0:T(8,128)S(1)}, f32[96,768]{1,0:T(8,128)S(1)}) custom-call(bf16[32,24,6272]{2,1,0:T(8,128)(2,1)} %pad_maximum_fusion.a_ref, bf16[32,96,768]{2,1,0:T(8,128)(2,1)} %bitcast.96), custom_call_target="tpu_custom_call" | custom-call | tf_op jit(solution)/shard_map/pallas_call | solution.py:430
  215.3 0.5 slice_bitcast_fusion
  215.9 0.7 fusion.85
  216.6 0.7 slice.104
  217.3 0.5 slice_bitcast_fusion.1
  217.8 0.7 copy.128
  (102 shorter events, 6.1 us)
Async XLA Ops:
  2.4 0.9 copy-start
  79.6 5.2 %copy-start.11 = (f32[256]{0:T(256)}, f32[256]{0:T(256)S(1)}, u32[]{:S(2)}) copy-start(f32[256]{0:T(256)S(1)} %broadcast_multiply_fusion.5) | copy-start | bytes 3076
  80.9 0.6 copy-start.17
  85.2 2.4 %copy-start.8 = (bf16[2,128,12,64]{1,0,3,2:T(2,128)(2,1)}, bf16[2,128,12,64]{1,0,3,2:T(2,128)(2,1)S(1)}, u32[]{:S(2)}) copy-start(bf16[2,128,12,64]{1,0,3,2:T(2,128)(2,1)S(1)} %reshape.162) | copy-start | bytes 1179652
  85.7 4.2 %copy-start.2 = (bf16[2,128,12,64]{1,0,3,2:T(2,128)(2,1)}, bf16[2,128,12,64]{1,0,3,2:T(2,128)(2,1)S(1)}, u32[]{:S(2)}) copy-start(bf16[2,128,12,64]{1,0,3,2:T(2,128)(2,1)S(1)} %reshape.163) | copy-start | bytes 1179652
  87.6 0.6 copy-start.15
  88.2 2.2 %copy-start.1 = (bf16[256,768]{1,0:T(8,128)(2,1)S(1)}, bf16[256,768]{1,0:T(8,128)(2,1)}, u32[]{:S(2)}) copy-start(bf16[256,768]{1,0:T(8,128)(2,1)} %param.18) | copy-start | bytes 1179652
  93.0 15.3 %copy-start.21 = (f32[256]{0:T(256)}, f32[256]{0:T(256)S(1)}, u32[]{:S(2)}) copy-start(f32[256]{0:T(256)S(1)} %compare_convert_fusion) | copy-start | bytes 3076
  94.2 14.1 %copy-start.14 = (f32[256]{0:T(256)}, f32[256]{0:T(256)S(1)}, u32[]{:S(2)}) copy-start(f32[256]{0:T(256)S(1)} %broadcast_multiply_fusion.4) | copy-start | bytes 3076
  94.2 4.2 %slice-start.3 = ((s8[4718592]{0:T(1024)(128)(4,1)}), s8[4194304]{0:T(1024)(128)(4,1)S(1)}, s32[]{:S(2)}) async-start(s8[4718592]{0:T(1024)(128)(4,1)} %bitcast.120), calls=%async_computation.3 | async-start | bytes 8388608
  94.5 13.9 %copy-start.20 = (f32[256]{0:T(256)}, f32[256]{0:T(256)S(1)}, u32[]{:S(2)}) copy-start(f32[256]{0:T(256)S(1)} %add_rsqrt_fusion) | copy-start | bytes 3076
  94.5 4.0 %slice-start.4 = ((s8[4718592]{0:T(1024)(128)(4,1)}), s8[524288]{0:T(1024)(128)(4,1)S(1)}, s32[]{:S(2)}) async-start(s8[4718592]{0:T(1024)(128)(4,1)} %bitcast.120), calls=%async_computation.4 | async-start | bytes 1048576
  98.5 2.8 %copy-start.23 = (f32[256,3072]{1,0:T(8,128)}, f32[256,3072]{1,0:T(8,128)S(1)}, u32[]{:S(2)}) copy-start(f32[256,3072]{1,0:T(8,128)S(1)} %fusion.5) | copy-start | bytes 9437188
  98.5 2.8 %copy-start.6 = (bf16[256,768]{1,0:T(8,128)(2,1)S(1)}, bf16[256,768]{1,0:T(8,128)(2,1)}, u32[]{:S(2)}) copy-start(bf16[256,768]{1,0:T(8,128)(2,1)} %param.19) | copy-start | bytes 1179652
  98.5 7.7 %slice-start = ((s8[9633792]{0:T(1024)(128)(4,1)}), s8[4194304]{0:T(1024)(128)(4,1)S(1)}, s32[]{:S(2)}) async-start(s8[9633792]{0:T(1024)(128)(4,1)} %bitcast.107), calls=%async_computation | async-start | bytes 8388608
  98.5 7.6 %slice-start.1 = ((s8[9633792]{0:T(1024)(128)(4,1)}), s8[4194304]{0:T(1024)(128)(4,1)S(1)}, s32[]{:S(2)}) async-start(s8[9633792]{0:T(1024)(128)(4,1)} %bitcast.107), calls=%async_computation.1 | async-start | bytes 8388608
  101.2 4.9 %slice-start.2 = ((s8[9633792]{0:T(1024)(128)(4,1)}), s8[1245184]{0:T(1024)(128)(4,1)S(1)}, s32[]{:S(2)}) async-start(s8[9633792]{0:T(1024)(128)(4,1)} %bitcast.107), calls=%async_computation.2 | async-start | bytes 2490368
  106.1 2.2 copy-start.5
  110.1 2.1 copy-start.9
  110.1 2.2 copy-start.4
  110.1 2.1 copy-start.16
  112.3 1.2 copy-start.3
  112.7 2.0 copy-start.10
  114.6 1.2 copy-start.12
  114.7 1.2 copy-start.18
  135.9 3.5 %copy-start.13 = (f32[256]{0:T(256)S(1)}, f32[256]{0:T(256)}, u32[]{:S(2)}) copy-start(f32[256]{0:T(256)} %copy-done.11) | copy-start | bytes 3076
  135.9 3.5 %copy-start.19 = (f32[256]{0:T(256)S(1)}, f32[256]{0:T(256)}, u32[]{:S(2)}) copy-start(f32[256]{0:T(256)} %copy-done.17) | copy-start | bytes 3076
  140.7 4.3 %copy-start.7 = (bf16[256,768]{1,0:T(8,128)(2,1)S(1)}, bf16[256,768]{1,0:T(8,128)(2,1)}, u32[]{:S(2)}) copy-start(bf16[256,768]{1,0:T(8,128)(2,1)} %param.19) | copy-start | bytes 1179652
  140.7 4.3 %copy-start.22 = (f32[256]{0:T(256)S(1)}, f32[256]{0:T(256)}, u32[]{:S(2)}) copy-start(f32[256]{0:T(256)} %copy-done.21) | copy-start | bytes 3076
  140.7 4.3 %copy-start.24 = (f32[256,3072]{1,0:T(8,128)S(1)}, f32[256,3072]{1,0:T(8,128)}, u32[]{:S(2)}) copy-start(f32[256,3072]{1,0:T(8,128)} %copy-done.23) | copy-start | bytes 9437188
